TPU v7x, 32 devices: a whole 2x2x4 slice. The times are simulated.
32 devices in a mesh: groups: 2 (over x), ffn: 16 (over z, y, core).
Axes of the slice: x: 2, y: 2, z: 4, core: 2. Of those that a mesh axis runs over, the one named last changes fastest.
Arguments:
- queries: bfloat16 [32, 2, 32, 1024], P(('groups', 'ffn')), parts along dimension 0, may hold values from -100 to 100
- block_kv: bfloat16 [32, 2, 32, 256], P(('groups', 'ffn')), parts along dimension 0, may hold values from -4 to 4
- cache_kv: bfloat16 [32, 2, 1536, 256], P(('groups', 'ffn')), parts along dimension 0, may hold values from -6 to 6
- prefix_len: int32 [8], P('groups'), parts along dimension 0, may hold values from 1 to 1536, as said below
- block_valid: int32 [8], P('groups'), parts along dimension 0, may hold values from 16 to 32, as said below
- resid: bfloat16 [32, 2, 32, 1024], P(('groups', 'ffn')), parts along dimension 0, may hold values from -6 to 6
- norm_gain: float32 [8192], replicated, may hold values from 0.25 to 1.75
- w_gate: bfloat16 [8192, 14336], P(None, 'ffn'), may hold values from -0.0625 to 0.0625
- w_up: bfloat16 [8192, 14336], P(None, 'ffn'), may hold values from -0.0625 to 0.0625
- w_down: bfloat16 [14336, 8192], P('ffn'), may hold values from -0.0625 to 0.0625
Outputs:
- layer_out: bfloat16 [32, 2, 32, 1024], P(('groups', 'ffn')), parts along dimension 0
There are 2 independent parts, one for each index of `groups`. A program takes and returns all parts, laid end to end along the dimension named above; an argument that names none is the same for every part. Nothing has to cross between parts.
Inputs may be any that keep to these rules, and one draw needn't show every extreme that they name: `prefix_len`: some request has exactly 1536. `block_valid`: some request has exactly 32.
All inputs are finite; a program needn't handle non-finite values.
Results may differ from a plain program's by a relative error of at most 0.0061.
Values may be sent and summed in bfloat16 or wider, within the bound.
A program may use at most 128 MiB of HBM per device.

v0:
```python
import jax
import jax.numpy as jnp
from jax import lax
from jax.sharding import PartitionSpec as P

KVH = 8


epsilon = 1e-05


def attend_local(queries, block_kv, cache_kv, prefix_here, valid_here):
    slot_count = queries.shape[0]
    request_count = queries.shape[1]
    block_len = queries.shape[2]
    cache_len = cache_kv.shape[2]
    head_size = block_kv.shape[3] // 2
    query_count = queries.shape[3] // head_size
    keys_all = jnp.concatenate([cache_kv[..., :head_size], block_kv[..., :head_size]], axis=2)
    values_all = jnp.concatenate([cache_kv[..., head_size:], block_kv[..., head_size:]], axis=2)
    positions = jnp.arange(cache_len + block_len)
    visible = jnp.where(
        positions[None, None, :] < cache_len,
        positions[None, None, :] < prefix_here[:, :, None],
        positions[None, None, :] - cache_len < valid_here[:, :, None],
    )
    query_heads = queries.reshape(slot_count, request_count, block_len, query_count, head_size)
    scores = jnp.einsum(
        "srbgd,srkd->srgbk", query_heads, keys_all, preferred_element_type=jnp.float32
    )
    scores = scores * (1.0 / jnp.sqrt(jnp.float32(head_size)))
    masked = jnp.where(visible[:, :, None, None, :], scores, jnp.float32(-1e30))
    peak = jnp.max(masked, axis=-1, keepdims=True)
    exps = jnp.exp(masked - peak)
    totals = jnp.sum(exps, axis=-1, keepdims=True)
    probability = (exps / totals).astype(jnp.bfloat16)
    mixed = jnp.einsum(
        "srgbk,srkd->srbgd", probability, values_all, preferred_element_type=jnp.float32
    )
    return mixed.reshape(slot_count, request_count, block_len, query_count * head_size)


def body(
    queries, block_kv, cache_kv, prefix_len, block_valid, resid, norm_gain, w_gate, w_up, w_down
):
    axis_count = lax.axis_size("ffn")
    device_index = lax.axis_index("ffn")
    group_count = axis_count // KVH
    group_index = device_index // KVH
    request_count = queries.shape[1]
    block_len = queries.shape[2]
    width = queries.shape[3]
    model_width = KVH * width
    hidden_here = w_gate.shape[1]
    prefix_here = lax.dynamic_slice_in_dim(prefix_len, group_index * request_count, request_count)[
        None, :
    ]
    valid_here = lax.dynamic_slice_in_dim(block_valid, group_index * request_count, request_count)[
        None, :
    ]
    attended = attend_local(queries, block_kv, cache_kv, prefix_here, valid_here)
    mid_state = (resid.astype(jnp.float32) + attended).astype(jnp.bfloat16)
    gathered = lax.all_gather(mid_state, "ffn", axis=0, tiled=True)
    mid_split = gathered.astype(jnp.float32).reshape(
        group_count, KVH, request_count, block_len, width
    )
    mean_square = jnp.sum(mid_split * mid_split, axis=(1, 4)) / model_width
    inv_root = lax.rsqrt(mean_square + epsilon)
    gain_split = norm_gain.reshape(KVH, width)[None, :, None, None, :]
    normed_split = (mid_split * inv_root[:, None, :, :, None] * gain_split).astype(jnp.bfloat16)
    gate_split = w_gate.reshape(KVH, width, hidden_here)
    up_split = w_up.reshape(KVH, width, hidden_here)
    gate_proj = jnp.einsum(
        "ghrbc,hcf->grbf", normed_split, gate_split, preferred_element_type=jnp.float32
    )
    up_proj = jnp.einsum(
        "ghrbc,hcf->grbf", normed_split, up_split, preferred_element_type=jnp.float32
    )
    hidden = (jax.nn.silu(gate_proj) * up_proj).astype(jnp.bfloat16)
    down_split = w_down.reshape(hidden_here, KVH, width)
    partial_value = jnp.einsum(
        "grbf,fhc->ghrbc", hidden, down_split, preferred_element_type=jnp.float32
    )
    partial_value = partial_value.reshape(axis_count, request_count, block_len, width)
    ffn_sum = lax.psum_scatter(partial_value, "ffn", scatter_dimension=0, tiled=True)
    return (mid_state.astype(jnp.float32) + ffn_sum).astype(jnp.bfloat16)


def solution(mesh):
    in_specs = (
        P(("groups", "ffn"), None, None, None),
        P(("groups", "ffn"), None, None, None),
        P(("groups", "ffn"), None, None, None),
        P("groups"),
        P("groups"),
        P(("groups", "ffn"), None, None, None),
        P(),
        P(None, "ffn"),
        P(None, "ffn"),
        P("ffn", None),
    )
    out_specs = P(("groups", "ffn"), None, None, None)
    return jax.shard_map(body, mesh=mesh, in_specs=in_specs, out_specs=out_specs, check_vma=False)
```

profile of v0, /device:TPU:0, one launch (start us, length us, event | category | flops | bytes accessed | tf_op | source)
XLA Modules:
  0.0 176.3 jit_solution(2345486890836359213)
XLA Ops:
  6.5 0.0 all-gather.2.cloned.1.call-start
  6.6 0.7 dynamic_slice.6
  7.3 0.7 dynamic_slice.7
  8.0 0.7 fusion.30
  8.8 0.9 copy.77
  9.7 1.5 fusion.29
  11.2 0.1 compare_select_fusion
  11.3 0.8 bitcast_reduce_fusion
  12.0 0.6 fusion.5
  12.6 0.0 copy-start.2
  12.6 0.0 copy-start.3
  12.7 0.9 fusion.13
  13.6 0.2 copy.56
  13.8 0.0 copy-done.2
  13.8 0.7 fusion.23
  14.5 0.0 all-gather.2.cloned.1.call-update
  14.5 0.0 reduce-scatter.2.cloned.1.call-start
  14.6 0.0 copy-done.3
  14.6 16.7 %copy.78 = bf16[112,8,8,1024]{3,2,1,0:T(8,128)(2,1)} copy(bf16[112,8,8,1024]{3,1,2,0:T(8,128)(2,1)} %bitcast.91) | data formatting | bytes 29360128
  31.3 27.5 %all-gather.2.cloned.1.call-done = bf16[16,2,32,1024]{3,2,1,0:T(8,128)(2,1)} async-done(((bf16[1,2,32,1024]{3,2,1,0:T(8,128)(2,1)}), bf16[16,2,32,1024]{3,2,1,0:T(8,128)(2,1)}) %all-gather.2.cloned.1.call-update) | async-done | bytes 2097168 | tf_op jit(solution)/shard_map/all_gather | solution.py:63
  58.8 2.1 %multiply_reduce_fusion = f32[16,2,32]{2,1,0:T(2,128)S(1)} fusion(bf16[16,2,32,1024]{3,2,1,0:T(8,128)(2,1)} %all-gather.2.cloned.1.call-done), kind=kLoop, calls=%fused_computation.5 | loop fusion | flops 3144704 | bytes 2101248 | tf_op jit(solution)/shard_map/reduce_sum | solution.py:67
  60.9 0.0 copy-start
  60.9 0.0 slice-start
  60.9 0.0 slice-start.1
  60.9 8.3 %convolution_bitcast_fusion.1 = f32[2,2,32,896]{3,2,1,0:T(8,128)S(1)} fusion(bf16[8,1024,896,1,1]{2,1,0,4,3:T(8,128)(2,1)} %bitcast.97, f32[8,1024]{1,0:T(8,128)S(1)} %mul.50, f32[2,2,32]{2,1,0:T(2,128)S(1)} %copy.60, bf16[2,8,2,32,1024]{4,3,2,1,0:T(8,128)(2,1)} %bitcast.92), kind=kOutput, calls=%fused_computation.17 | convolution fusion | flops 1883242496 | bytes 17269248 | tf_op jit(solution)/shard_map/ghrbc,hcf->grbf/dot_general | solution.py:73
  69.3 0.0 copy-done
  69.3 0.0 slice-start.2
  69.3 0.0 slice-start.3
  69.3 7.8 %fusion.16 = bf16[2,2,32,896,1]{3,2,4,1,0:T(8,128)(2,1)S(1)} fusion(bf16[8,1024,896,1,1]{2,1,0,4,3:T(8,128)(2,1)} %bitcast.98, f32[2,2,32,896]{3,2,1,0:T(8,128)S(1)} %convolution_bitcast_fusion.1, f32[8,1024]{1,0:T(8,128)S(1)} %mul.50, f32[2,2,32]{2,1,0:T(2,128)S(1)} %copy.60, bf16[2,8,2,32,1024]{4,3,2,1,0:T(8,128)(2,1)S(1)} %bitcast.93), kind=kOutput, calls=%fused_computation.20 | convolution fusion | flops 1883930624 | bytes 17498624 | tf_op jit(solution)/shard_map/ghrbc,hcf->grbf/dot_general | solution.py:76
  77.1 0.0 slice-done
  77.1 0.0 slice-done.1
  77.1 0.0 slice-done.2
  77.1 0.0 slice-done.3
  77.1 17.0 %fusion.6 = f32[2,8,2,32,1024]{4,3,1,2,0:T(8,128)S(1)} fusion(bf16[2,2,32,896,1]{3,2,4,1,0:T(8,128)(2,1)S(1)} %fusion.16, bf16[896,8,1024,1,1]{2,1,0,4,3:T(8,128)(2,1)S(1)} %bitcast.89), kind=kOutput, calls=%fused_computation.12 | convolution fusion | flops 1879048192 | bytes 19103744 | tf_op jit(solution)/shard_map/grbf,fhc->ghrbc/dot_general | solution.py:81
  94.1 2.3 %copy.63 = f32[2,8,2,32,1024]{4,3,2,1,0:T(8,128)} copy(f32[2,8,2,32,1024]{4,3,1,2,0:T(8,128)S(1)} %fusion.6) | data formatting | bytes 8388608 | tf_op jit(solution)/shard_map/grbf,fhc->ghrbc/transpose | solution.py:81
  96.4 0.0 copy-start.1
  96.4 0.0 reduce-scatter.2.cloned.1.call-update
  96.4 71.4 %reduce-scatter.2.cloned.1.call-done = f32[1,2,32,1024]{3,2,1,0:T(8,128)} async-done(((f32[16,2,32,1024]{3,2,1,0:T(8,128)}), f32[1,2,32,1024]{3,2,1,0:T(8,128)}) %reduce-scatter.2.cloned.1.call-update) | async-done | bytes 262160 | tf_op jit(solution)/shard_map/reduce_scatter | solution.py:85
  167.8 0.0 copy-done.1
  167.8 1.6 add_convert_fusion
  (7 shorter events, 0.1 us)
Async XLA Ops:
  6.5 52.2 %all-gather.2.cloned.1.call-start = ((), (), s32[]{:S(2)}) async-start(), calls=%async_computation.1 | async-start | bytes 2228224 | tf_op jit(solution)/shard_map/all_gather | solution.py:63
  12.6 1.1 copy-start.2
  12.6 1.9 %copy-start.3 = (f32[8192]{0:T(1024)S(1)}, f32[8192]{0:T(1024)}, u32[]{:S(2)}) copy-start(f32[8192]{0:T(1024)} %param.16) | copy-start | bytes 98308
  14.5 153.3 %reduce-scatter.2.cloned.1.call-start = ((), (), s32[]{:S(2)}) async-start(), calls=%async_computation.2 | async-start | bytes 4456448 | tf_op jit(solution)/shard_map/reduce_scatter | solution.py:85
  60.9 8.4 %copy-start = (bf16[16,2,32,1024]{3,2,1,0:T(8,128)(2,1)S(1)}, bf16[16,2,32,1024]{3,2,1,0:T(8,128)(2,1)}, u32[]{:S(2)}) copy-start(bf16[16,2,32,1024]{3,2,1,0:T(8,128)(2,1)} %all-gather.2.cloned.1.call-done) | copy-start | bytes 6291460
  60.9 16.2 %slice-start = ((s8[14680064]{0:T(1024)(128)(4,1)}), s8[4194304]{0:T(1024)(128)(4,1)S(1)}, s32[]{:S(2)}) async-start(s8[14680064]{0:T(1024)(128)(4,1)} %bitcast.87), calls=%async_computation.3 | async-start | bytes 8388608
  60.9 16.2 %slice-start.1 = ((s8[14680064]{0:T(1024)(128)(4,1)}), s8[4194304]{0:T(1024)(128)(4,1)S(1)}, s32[]{:S(2)}) async-start(s8[14680064]{0:T(1024)(128)(4,1)} %bitcast.87), calls=%async_computation.4 | async-start | bytes 8388608
  69.3 7.8 %slice-start.2 = ((s8[14680064]{0:T(1024)(128)(4,1)}), s8[4194304]{0:T(1024)(128)(4,1)S(1)}, s32[]{:S(2)}) async-start(s8[14680064]{0:T(1024)(128)(4,1)} %bitcast.87), calls=%async_computation.5 | async-start | bytes 8388608
  69.3 7.8 %slice-start.3 = ((s8[14680064]{0:T(1024)(128)(4,1)}), s8[2097152]{0:T(1024)(128)(4,1)S(1)}, s32[]{:S(2)}) async-start(s8[14680064]{0:T(1024)(128)(4,1)} %bitcast.87), calls=%async_computation.6 | async-start | bytes 4194304
  96.4 71.4 %copy-start.1 = (bf16[1,2,32,1024]{3,2,1,0:T(8,128)(2,1)S(1)}, bf16[1,2,32,1024]{3,2,1,0:T(8,128)(2,1)}, u32[]{:S(2)}) copy-start(bf16[1,2,32,1024]{3,2,1,0:T(8,128)(2,1)} %fusion.23) | copy-start | bytes 393220
Sparse Core Ops, SparseCore 0:
  14.6 44.0 all-gather.1
  96.5 71.2 reduce-scatter.1
where the time goes:
time: 177 us; the launch traced here: 176 us
  waiting for transfers between devices  98.9 us (56%)
  matrix products  34.8 us (20%)
  local copies, waits for them, and re-layouts  23.7 us (13%)
  between operations  13.6 us (8%)
  other arithmetic  5.15 us (3%)
    reduce_scatter x1, waiting for transfers between devices, body(): lax.psum_scatter(partial_value, 'ffn', scatter_dimension=0, tiled=True)  71.4 us
    all_gather x1, waiting for transfers between devices, body(): gathered = lax.all_gather(mid_state, 'ffn', axis=0, tiled=True)  27.5 us
    unnamed x18, local copies, waits for them, and re-layouts  17.6 us
    dot_general x1, matrix products, body(): jnp.einsum('grbf,fhc->ghrbc', hidden, down_split, preferred_element_type=...  17 us
    dot_general x1, matrix products, body(): jnp.einsum('ghrbc,hcf->grbf', normed_split, gate_split, preferred_element...  8.34 us
    dot_general x1, matrix products, body(): jnp.einsum('ghrbc,hcf->grbf', normed_split, up_split, preferred_element_t...  7.78 us
  transfers between devices with their start and end apart: 2, of which 2 were waited for; matrix products, arithmetic and copies ran while one was open for 9% of the time, Pallas kernels for 0%

commit v1 on v0

v1 whole, which is shorter than its diff:
```python
import functools

import jax
import jax.numpy as jnp
from jax import lax
from jax.experimental import pallas as pl
from jax.experimental.pallas import tpu as pltpu
from jax.sharding import PartitionSpec as P

KVH = 8
CORES = 2

epsilon = 1e-05


def ring_is_snake(mesh):
    row = mesh.devices.reshape(mesh.shape["groups"], mesh.shape["ffn"])[0]
    chips = [getattr(row[i], "coords", None) for i in range(0, len(row), CORES)]
    if len(chips) < 4 or any(c is None for c in chips):
        return False
    return any(
        all(c[axis] == chips[i % 2][axis] for i, c in enumerate(chips))
        and chips[0][axis] != chips[1][axis]
        for axis in range(len(chips[0]))
    )


def layer_kernel(
    ring,
    snake,
    q_ref,
    bkv_ref,
    cache_hbm,
    prefix_ref,
    valid_ref,
    resid_ref,
    gain_ref,
    wg_hbm,
    wu_hbm,
    wd_hbm,
    out_ref,
    cache,
    wg,
    wu,
    wd,
    xg,
    acc_g,
    acc_u,
    sumsq,
    hid,
    csum,
    psend,
    precv,
    rsend,
    rrecv,
    lsend,
    lrecv,
    cache_sem,
    w_sem,
    ag_recv,
    ag_right,
    ag_left,
    ag_pair,
    p_ssem,
    p_rsem,
    r_ssem,
    r_rsem,
    l_ssem,
    l_rsem,
):
    reqs, block_len, width = q_ref.shape
    cache_len = cache.shape[1]
    head_size = cache.shape[2] // 2
    heads = width // head_size
    hidden_here = wg.shape[1]
    model_width = KVH * width
    groups = acc_g.shape[0]
    rows = reqs * block_len
    pairs = KVH // CORES
    half = ring // 2
    me = lax.axis_index("ffn")
    core = me % CORES
    chip = me // CORES
    if snake:
        here = (1 - chip % 2) * (chip // 2) + (chip % 2) * (ring - 1 - chip // 2)
    else:
        here = chip

    def chip_at(offset):
        place = (here + offset + ring) % ring
        if not snake:
            return place
        back = place // half
        return (1 - back) * (2 * place) + back * (2 * (ring - 1 - place) + 1)

    partner = chip * CORES + (1 - core)
    right = chip_at(1) * CORES + core
    left = chip_at(-1) * CORES + core

    barrier = pltpu.get_barrier_semaphore()
    for other in (partner, right, left):
        pl.semaphore_signal(
            barrier, inc=1, device_id={"ffn": other}, device_id_type=pl.DeviceIdType.MESH
        )

    cache_copies = [
        pltpu.make_async_copy(cache_hbm.at[r], cache.at[r], cache_sem.at[r]) for r in range(reqs)
    ]
    for copy in cache_copies:
        copy.start()
    weight_copies = []
    for w, (source, target) in enumerate(((wg_hbm, wg), (wu_hbm, wu))):
        for h in range(KVH):
            span = pl.ds(h * width, width)
            weight_copies.append(
                pltpu.make_async_copy(source.at[span], target.at[span], w_sem.at[w, h])
            )
    down_copies = []
    for h in range(KVH):
        span = pl.ds(h * width, width)
        down_copies.append(
            pltpu.make_async_copy(wd_hbm.at[:, span], wd.at[:, span], w_sem.at[2, h])
        )
    for copy in weight_copies + down_copies:
        copy.start()

    def send(source, target, ssem, rsem, device):
        return pltpu.make_async_remote_copy(
            src_ref=source,
            dst_ref=target,
            send_sem=ssem,
            recv_sem=rsem,
            device_id={"ffn": device},
            device_id_type=pl.DeviceIdType.MESH,
        )

    def to_right(s, i):
        return send(xg.at[s, i], xg.at[s, i], ag_right.at[s, i], ag_recv.at[s, i], right)

    def to_left(s, i):
        return send(xg.at[s, i], xg.at[s, i], ag_left.at[s, i], ag_recv.at[s, i], left)

    def to_pair(s, i):
        return send(xg.at[s, i], xg.at[s, i], ag_pair.at[s, i], ag_recv.at[s, i], partner)

    def goes_right(i):
        return i < reqs // 2

    group = me // KVH
    scale = 1.0 / (head_size**0.5)
    for r in range(reqs):
        cache_copies[r].wait()
        query = q_ref[r]
        stacked = jnp.concatenate(
            [query[:, h * head_size : (h + 1) * head_size] for h in range(heads)], axis=0
        )
        contract = (((1,), (1,)), ((), ()))
        far = lax.dot_general(
            stacked, cache[r, :, :head_size], contract, preferred_element_type=jnp.float32
        )
        near = lax.dot_general(
            stacked, bkv_ref[r, :, :head_size], contract, preferred_element_type=jnp.float32
        )
        seen = prefix_ref[group * reqs + r]
        live = valid_ref[group * reqs + r]
        far_at = lax.broadcasted_iota(jnp.int32, (1, cache_len), 1)
        near_at = lax.broadcasted_iota(jnp.int32, (1, block_len), 1)
        far = jnp.where(far_at < seen, far * scale, -1e30)
        near = jnp.where(near_at < live, near * scale, -1e30)
        peak = jnp.maximum(
            jnp.max(far, axis=-1, keepdims=True), jnp.max(near, axis=-1, keepdims=True)
        )
        far = jnp.exp(far - peak)
        near = jnp.exp(near - peak)
        total = jnp.sum(far, axis=-1, keepdims=True) + jnp.sum(near, axis=-1, keepdims=True)
        inverse = 1.0 / total
        mixed = jnp.dot(
            (far * inverse).astype(jnp.bfloat16),
            cache[r, :, head_size:],
            preferred_element_type=jnp.float32,
        ) + jnp.dot(
            (near * inverse).astype(jnp.bfloat16),
            bkv_ref[r, :, head_size:],
            preferred_element_type=jnp.float32,
        )
        side = jnp.concatenate(
            [mixed[h * block_len : (h + 1) * block_len] for h in range(heads)], axis=1
        )
        xg[me, r] = (resid_ref[r].astype(jnp.float32) + side).astype(jnp.bfloat16)
        if r == 0:
            pl.semaphore_wait(barrier, 3)
        to_right(me, r).start()
        to_left(me, r).start()
        to_pair(me, r).start()

    acc_g[...] = jnp.zeros_like(acc_g)
    acc_u[...] = jnp.zeros_like(acc_u)
    sumsq[...] = jnp.zeros_like(sumsq)

    def absorb(s):
        g = s // KVH
        span = pl.ds(pl.multiple_of((s % KVH) * width, width), width)
        block = xg[s].reshape(rows, width).astype(jnp.float32)
        square = block * block
        folded = square[:, :head_size]
        for h in range(1, heads):
            folded = folded + square[:, h * head_size : (h + 1) * head_size]
        sumsq[g] += folded
        scaled = (block * gain_ref[:, span]).astype(jnp.bfloat16)
        acc_g[g] += jnp.dot(scaled, wg[span, :], preferred_element_type=jnp.float32)
        acc_u[g] += jnp.dot(scaled, wu[span, :], preferred_element_type=jnp.float32)

    def absorb_pair(s):
        for i in range(reqs):
            to_pair(s, i).wait_recv()
        absorb(s)

    def pass_on(t, last):
        from_left = chip_at(-t) * CORES + core
        from_right = chip_at(t) * CORES + core
        for i in range(reqs):
            to_right(from_left, i).wait_recv()
            if not last or goes_right(i):
                to_right(from_left, i).start()
            to_pair(from_left, i).start()
            to_left(from_right, i).wait_recv()
            if not last or not goes_right(i):
                to_left(from_right, i).start()
            to_pair(from_right, i).start()

    def absorb_step(t):
        absorb(chip_at(-t) * CORES + core)
        absorb(chip_at(t) * CORES + core)
        absorb_pair(chip_at(-t) * CORES + 1 - core)
        absorb_pair(chip_at(t) * CORES + 1 - core)

    pass_on(1, half == 2)
    for copy in weight_copies:
        copy.wait()
    absorb(me)
    absorb_pair(partner)
    absorb_step(1)

    def middle(t, carry):
        pass_on(t, False)
        absorb_step(t)
        return carry

    if half > 2:
        lax.fori_loop(2, half - 1, middle, 0)
        pass_on(half - 1, True)
        absorb_step(half - 1)
    far_chip = chip_at(half)
    for i in range(reqs):
        (to_right if goes_right(i) else to_left)(far_chip * CORES + core, i).wait_recv()
        to_pair(far_chip * CORES + core, i).start()
    absorb(far_chip * CORES + core)
    absorb_pair(far_chip * CORES + 1 - core)

    for g in range(groups):
        mean_square = jnp.sum(sumsq[g], axis=-1, keepdims=True) / model_width
        root = lax.rsqrt(mean_square + epsilon)
        gate = acc_g[g] * root
        up = acc_u[g] * root
        hid[g * rows : (g + 1) * rows, :] = (gate * jax.nn.sigmoid(gate) * up).astype(jnp.bfloat16)

    for copy in down_copies:
        copy.wait()

    def pair_copy(k):
        return send(psend.at[k], precv.at[k], p_ssem.at[k], p_rsem.at[k], partner)

    def column_of(k, parity):
        return pl.ds(pl.multiple_of((k * CORES + parity) * width, width), width)

    def give(j, carry):
        k = (far_chip + j) % pairs
        share = jnp.dot(
            hid[...], wd[:, column_of(k, 1 - core)], preferred_element_type=jnp.float32
        )
        psend[k] = share.astype(jnp.bfloat16).reshape(groups, reqs, block_len, width)
        pair_copy(k).start()
        return carry

    def keep(j, carry):
        k = (far_chip + j) % pairs
        share = jnp.dot(hid[...], wd[:, column_of(k, core)], preferred_element_type=jnp.float32)
        pair_copy(k).wait_recv()
        csum[k] = share.reshape(groups, reqs, block_len, width) + precv[k].astype(jnp.float32)
        return carry

    lax.fori_loop(0, pairs, give, 0)
    lax.fori_loop(0, pairs, keep, 0)

    def right_copy(t, i):
        return send(rsend.at[t, i], rrecv.at[t, i], r_ssem.at[t, i], r_rsem.at[t, i], right)

    def left_copy(t, i):
        return send(lsend.at[t, i], lrecv.at[t, i], l_ssem.at[t, i], l_rsem.at[t, i], left)

    sent = []
    for t in range(half, 0, -1):
        for i in range(reqs):
            for copy_of, out_buf, in_buf, offset, first in (
                (right_copy, rsend, rrecv, t, goes_right(i)),
                (left_copy, lsend, lrecv, -t, not goes_right(i)),
            ):
                if t == half and not first:
                    continue
                target = chip_at(offset)
                value = csum[target % pairs, target // pairs, i]
                if t < half - 1 or (t == half - 1 and first):
                    copy_of(t, i).wait_recv()
                    value = value + in_buf[t, i].astype(jnp.float32)
                out_buf[t - 1, i] = value.astype(jnp.bfloat16)
                copy_of(t - 1, i).start()
                sent.append(copy_of(t - 1, i))
    for i in range(reqs):
        right_copy(0, i).wait_recv()
        left_copy(0, i).wait_recv()
        value = csum[chip % pairs, chip // pairs, i]
        value = value + rrecv[0, i].astype(jnp.float32) + lrecv[0, i].astype(jnp.float32)
        out_ref[i] = (xg[me, i].astype(jnp.float32) + value).astype(jnp.bfloat16)

    for copy in sent:
        copy.wait_send()

    def pair_sent(k, carry):
        pair_copy(k).wait_send()
        return carry

    lax.fori_loop(0, pairs, pair_sent, 0)

    def gather_sent(t, carry):
        for i in range(reqs):
            to_right(chip_at(-t) * CORES + core, i).wait_send()
            to_pair(chip_at(-t) * CORES + core, i).wait_send()
            to_left(chip_at(t) * CORES + core, i).wait_send()
            to_pair(chip_at(t) * CORES + core, i).wait_send()
        return carry

    for i in range(reqs):
        to_right(me, i).wait_send()
        to_left(me, i).wait_send()
        to_pair(me, i).wait_send()
        to_pair(far_chip * CORES + core, i).wait_send()
        (to_right(chip_at(1 - half) * CORES + core, i) if goes_right(i) else to_left(
            chip_at(half - 1) * CORES + core, i
        )).wait_send()
        to_pair(chip_at(1 - half) * CORES + core, i).wait_send()
        to_pair(chip_at(half - 1) * CORES + core, i).wait_send()
    lax.fori_loop(1, half - 1, gather_sent, 0)


def body(
    snake,
    queries,
    block_kv,
    cache_kv,
    prefix_len,
    block_valid,
    resid,
    norm_gain,
    w_gate,
    w_up,
    w_down,
):
    count = lax.axis_size("ffn")
    ring = count // CORES
    half = ring // 2
    _, reqs, block_len, width = queries.shape
    hidden_here = w_gate.shape[1]
    groups = count // KVH
    rows = reqs * block_len
    pairs = KVH // CORES
    lanes = block_kv.shape[3] // 2
    bf16, f32 = jnp.bfloat16, jnp.float32
    vmem = pl.BlockSpec(memory_space=pltpu.VMEM)
    smem = pl.BlockSpec(memory_space=pltpu.SMEM)
    hbm = pl.BlockSpec(memory_space=pl.ANY)
    dma = pltpu.SemaphoreType.DMA
    flops = 2 * groups * rows * KVH * width * hidden_here * 3
    out = pl.pallas_call(
        functools.partial(layer_kernel, ring, snake),
        out_shape=jax.ShapeDtypeStruct((reqs, block_len, width), bf16),
        in_specs=[vmem, vmem, hbm, smem, smem, vmem, vmem, hbm, hbm, hbm],
        out_specs=vmem,
        scratch_shapes=[
            pltpu.VMEM(cache_kv.shape[1:], bf16),
            pltpu.VMEM(w_gate.shape, bf16),
            pltpu.VMEM(w_up.shape, bf16),
            pltpu.VMEM(w_down.shape, bf16),
            pltpu.VMEM((count, reqs, block_len, width), bf16),
            pltpu.VMEM((groups, rows, hidden_here), f32),
            pltpu.VMEM((groups, rows, hidden_here), f32),
            pltpu.VMEM((groups, rows, lanes), f32),
            pltpu.VMEM((groups * rows, hidden_here), bf16),
            pltpu.VMEM((pairs, groups, reqs, block_len, width), f32),
            pltpu.VMEM((pairs, groups, reqs, block_len, width), bf16),
            pltpu.VMEM((pairs, groups, reqs, block_len, width), bf16),
            pltpu.VMEM((half, reqs, block_len, width), bf16),
            pltpu.VMEM((half, reqs, block_len, width), bf16),
            pltpu.VMEM((half, reqs, block_len, width), bf16),
            pltpu.VMEM((half, reqs, block_len, width), bf16),
            dma((reqs,)),
            dma((3, KVH)),
            dma((count, reqs)),
            dma((count, reqs)),
            dma((count, reqs)),
            dma((count, reqs)),
            dma((pairs,)),
            dma((pairs,)),
            dma((half, reqs)),
            dma((half, reqs)),
            dma((half, reqs)),
            dma((half, reqs)),
        ],
        compiler_params=pltpu.CompilerParams(
            collective_id=0, has_side_effects=True, vmem_limit_bytes=62 * 1024 * 1024
        ),
        cost_estimate=pl.CostEstimate(
            flops=flops, bytes_accessed=6 * KVH * width * hidden_here, transcendentals=0
        ),
    )(
        queries[0],
        block_kv[0],
        cache_kv[0],
        prefix_len,
        block_valid,
        resid[0],
        norm_gain.reshape(1, -1),
        w_gate,
        w_up,
        w_down,
    )
    return out[None]


def solution(mesh):
    in_specs = (
        P(("groups", "ffn"), None, None, None),
        P(("groups", "ffn"), None, None, None),
        P(("groups", "ffn"), None, None, None),
        P("groups"),
        P("groups"),
        P(("groups", "ffn"), None, None, None),
        P(),
        P(None, "ffn"),
        P(None, "ffn"),
        P("ffn", None),
    )
    out_specs = P(("groups", "ffn"), None, None, None)
    return jax.shard_map(
        functools.partial(body, ring_is_snake(mesh)),
        mesh=mesh,
        in_specs=in_specs,
        out_specs=out_specs,
        check_vma=False,
    )
```

time: 177 us -> 60.5 us (0.34)
  waiting for transfers between devices: 98.9 us -> 0 us
  Pallas kernels: 0 us -> 58.7 us
  matrix products: 34.8 us -> 0 us
  local copies, waits for them, and re-layouts: 23.7 us -> 1.57 us
  between operations: 13.6 us -> 0.01 us
  other arithmetic: 5.15 us -> 0 us
    reduce_scatter x1 -> x0, waiting for transfers between devices: 71.4 us -> none  [body(): lax.psum_scatter(partial_value, 'ffn', scatter_dimension=0, tiled=True)]
    pallas_call x0 -> x1, Pallas kernels: none -> 58.7 us  [body(): pl.pallas_call(functools.partial(layer_kernel, ring, snake), out_shape=ja...]
    dot_general x5 -> x0, matrix products: 34.8 us -> none  [the longest x1 17 us: body(): jnp.einsum('grbf,fhc->ghrbc', hidden, down_split, preferred_element_type=...]
    all_gather x1 -> x0, waiting for transfers between devices: 27.5 us -> none  [body(): gathered = lax.all_gather(mid_state, 'ffn', axis=0, tiled=True)]
    unnamed x18 -> x1, local copies, waits for them, and re-layouts: 17.6 us -> 1.57 us
    reduce_sum x2 -> x0, other arithmetic: 2.69 us -> none  [the longest x1 2.07 us: body(): mean_square = jnp.sum(mid_split * mid_split, axis=(1, 4)) / model_width]
    transpose x2 -> x0, local copies, waits for them, and re-layouts: 2.41 us -> none  [the longest x1 2.25 us: body(): jnp.einsum('grbf,fhc->ghrbc', hidden, down_split, preferred_element_type=...]
    convert_element_type x2 -> x0, other arithmetic: 2.34 us -> none  [the longest x1 1.63 us: body(): return (mid_state.astype(jnp.float32) + ffn_sum).astype(jnp.bfloat16)]
  transfers between devices with their start and end apart: 2 -> 0, of which waited for: 2 -> 0; matrix products, arithmetic and copies ran while one was open for 9% -> 0% of each run, Pallas kernels for 0% -> 0%
where the time goes in v1:
time: 60.5 us; the launch traced here: 60.3 us
  Pallas kernels  58.7 us (97%)
  local copies, waits for them, and re-layouts  1.57 us (3%)
    pallas_call x1, Pallas kernels, body(): pl.pallas_call(functools.partial(layer_kernel, ring, snake), out_shape=ja...  58.7 us
    unnamed x1, local copies, waits for them, and re-layouts  1.57 us

profile of v1, /device:TPU:0, one launch (start us, length us, event | category | flops | bytes accessed | tf_op | source)
XLA Modules:
  0.0 60.3 jit_solution(14103704516883135172)
XLA Ops:
  0.0 58.7 %shard_map.100 = bf16[2,32,1024]{2,1,0:T(8,128)(2,1)} custom-call(bf16[2,32,1024]{2,1,0:T(8,128)(2,1)} %bitcast.8, bf16[2,32,256]{2,1,0:T(8,128)(2,1)} %bitcast.10, bf16[2,1536,256]{2,1,0:T(8,128)(2,1)} %bitcast.6, s32[4]{0:T(128)} %prefix_ref.1, s32[4]{0:T(128)} %valid_ref.1, bf16[2,32,1024]{2,1,0:T(8,128)(2,1)} %bitcast.9, f32[1,8192]{1,0:T(1,128)} %bitcast.11, ...), custom_call_target="tpu_custom_call" | custom-call | flops 5637144576 | bytes 44040192 | tf_op jit(solution)/shard_map/pallas_call | solution.py:383
  58.8 1.6 %copy.12 = bf16[1,2,32,1024]{3,2,1,0:T(8,128)(2,1)} copy(bf16[1,2,32,1024]{3,2,1,0:T(8,128)(2,1)} %bitcast.7) | data formatting | bytes 262144

commit v2 on v1

--- a/solution.py
+++ b/solution.py
@@ -1,4 +1,5 @@
 import functools
+import math
 
 import jax
 import jax.numpy as jnp
@@ -74,10 +75,11 @@
     heads = width // head_size
     hidden_here = wg.shape[1]
     model_width = KVH * width
-    groups = acc_g.shape[0]
     rows = reqs * block_len
+    groups = acc_g.shape[0] // rows
     pairs = KVH // CORES
     half = ring // 2
+    paired = snake and ring == 2 * pairs == 8 and groups == 2
     me = lax.axis_index("ffn")
     core = me % CORES
     chip = me // CORES
@@ -147,7 +149,7 @@
         return i < reqs // 2
 
     group = me // KVH
-    scale = 1.0 / (head_size**0.5)
+    scale = math.log2(math.e) / (head_size**0.5)
     for r in range(reqs):
         cache_copies[r].wait()
         query = q_ref[r]
@@ -165,13 +167,13 @@
         live = valid_ref[group * reqs + r]
         far_at = lax.broadcasted_iota(jnp.int32, (1, cache_len), 1)
         near_at = lax.broadcasted_iota(jnp.int32, (1, block_len), 1)
-        far = jnp.where(far_at < seen, far * scale, -1e30)
-        near = jnp.where(near_at < live, near * scale, -1e30)
+        far = jnp.where(far_at < seen, far, -1e30)
+        near = jnp.where(near_at < live, near, -1e30)
         peak = jnp.maximum(
             jnp.max(far, axis=-1, keepdims=True), jnp.max(near, axis=-1, keepdims=True)
         )
-        far = jnp.exp(far - peak)
-        near = jnp.exp(near - peak)
+        far = jnp.exp2((far - peak) * scale)
+        near = jnp.exp2((near - peak) * scale)
         total = jnp.sum(far, axis=-1, keepdims=True) + jnp.sum(near, axis=-1, keepdims=True)
         inverse = 1.0 / total
         mixed = jnp.dot(
@@ -193,26 +195,52 @@
         to_left(me, r).start()
         to_pair(me, r).start()
 
-    acc_g[...] = jnp.zeros_like(acc_g)
-    acc_u[...] = jnp.zeros_like(acc_u)
-    sumsq[...] = jnp.zeros_like(sumsq)
+    def fold(square):
+        folded = square[:, :head_size]
+        for h in range(1, square.shape[1] // head_size):
+            folded = folded + square[:, h * head_size : (h + 1) * head_size]
+        return folded
 
     def absorb(s):
-        g = s // KVH
+        mine = pl.ds(pl.multiple_of((s // KVH) * rows, rows), rows)
         span = pl.ds(pl.multiple_of((s % KVH) * width, width), width)
         block = xg[s].reshape(rows, width).astype(jnp.float32)
-        square = block * block
-        folded = square[:, :head_size]
-        for h in range(1, heads):
-            folded = folded + square[:, h * head_size : (h + 1) * head_size]
-        sumsq[g] += folded
+        sumsq[mine] += fold(block * block)
         scaled = (block * gain_ref[:, span]).astype(jnp.bfloat16)
-        acc_g[g] += jnp.dot(scaled, wg[span, :], preferred_element_type=jnp.float32)
-        acc_u[g] += jnp.dot(scaled, wu[span, :], preferred_element_type=jnp.float32)
-
-    def absorb_pair(s):
+        acc_g[mine] += jnp.dot(scaled, wg[span, :], preferred_element_type=jnp.float32)
+        acc_u[mine] += jnp.dot(scaled, wu[span, :], preferred_element_type=jnp.float32)
+
+    def absorb_heads(k, first=False):
+        span = pl.ds(pl.multiple_of(k * CORES * width, CORES * width), CORES * width)
+        block = jnp.concatenate(
+            [
+                jnp.concatenate(
+                    [xg[g * KVH + k * CORES + c].reshape(rows, width) for c in range(CORES)],
+                    axis=1,
+                )
+                for g in range(groups)
+            ],
+            axis=0,
+        ).astype(jnp.float32)
+        squares = fold(block * block)
+        scaled = (block * gain_ref[:, span]).astype(jnp.bfloat16)
+        gate = jnp.dot(scaled, wg[span, :], preferred_element_type=jnp.float32)
+        up = jnp.dot(scaled, wu[span, :], preferred_element_type=jnp.float32)
+        if first:
+            sumsq[...] = squares
+            acc_g[...] = gate
+            acc_u[...] = up
+        else:
+            sumsq[...] += squares
+            acc_g[...] += gate
+            acc_u[...] += up
+
+    def pair_arrived(s):
         for i in range(reqs):
             to_pair(s, i).wait_recv()
+
+    def absorb_pair(s):
+        pair_arrived(s)
         absorb(s)
 
     def pass_on(t, last):
@@ -234,35 +262,63 @@
         absorb_pair(chip_at(-t) * CORES + 1 - core)
         absorb_pair(chip_at(t) * CORES + 1 - core)
 
-    pass_on(1, half == 2)
-    for copy in weight_copies:
-        copy.wait()
-    absorb(me)
-    absorb_pair(partner)
-    absorb_step(1)
-
-    def middle(t, carry):
-        pass_on(t, False)
-        absorb_step(t)
-        return carry
-
-    if half > 2:
-        lax.fori_loop(2, half - 1, middle, 0)
-        pass_on(half - 1, True)
-        absorb_step(half - 1)
+    def from_far():
+        for i in range(reqs):
+            (to_right if goes_right(i) else to_left)(far_chip * CORES + core, i).wait_recv()
+            to_pair(far_chip * CORES + core, i).start()
+
     far_chip = chip_at(half)
-    for i in range(reqs):
-        (to_right if goes_right(i) else to_left)(far_chip * CORES + core, i).wait_recv()
-        to_pair(far_chip * CORES + core, i).start()
-    absorb(far_chip * CORES + core)
-    absorb_pair(far_chip * CORES + 1 - core)
-
-    for g in range(groups):
-        mean_square = jnp.sum(sumsq[g], axis=-1, keepdims=True) / model_width
-        root = lax.rsqrt(mean_square + epsilon)
-        gate = acc_g[g] * root
-        up = acc_u[g] * root
-        hid[g * rows : (g + 1) * rows, :] = (gate * jax.nn.sigmoid(gate) * up).astype(jnp.bfloat16)
+    other = 1 - core
+    k_own = chip % pairs
+    k_far = far_chip % pairs
+    if paired:
+        k_near = k_own + 1 - 2 * (k_own % 2)
+        k_next = pairs - 1 - k_near
+        pass_on(1, False)
+        pair_arrived(partner)
+        pass_on(2, False)
+        for t in (-1, 1, -2, 2):
+            pair_arrived(chip_at(t) * CORES + other)
+        for copy in weight_copies:
+            copy.wait()
+        absorb_heads(k_own, True)
+        pass_on(3, True)
+        for t in (-3, 3):
+            pair_arrived(chip_at(t) * CORES + other)
+        absorb_heads(k_near)
+        from_far()
+        absorb_heads(k_next)
+        pair_arrived(far_chip * CORES + other)
+        absorb_heads(k_far)
+    else:
+        acc_g[...] = jnp.zeros_like(acc_g)
+        acc_u[...] = jnp.zeros_like(acc_u)
+        sumsq[...] = jnp.zeros_like(sumsq)
+        pass_on(1, half == 2)
+        for copy in weight_copies:
+            copy.wait()
+        absorb(me)
+        absorb_pair(partner)
+        absorb_step(1)
+
+        def middle(t, carry):
+            pass_on(t, False)
+            absorb_step(t)
+            return carry
+
+        if half > 2:
+            lax.fori_loop(2, half - 1, middle, 0)
+            pass_on(half - 1, True)
+            absorb_step(half - 1)
+        from_far()
+        absorb(far_chip * CORES + core)
+        absorb_pair(far_chip * CORES + other)
+
+    mean_square = jnp.sum(sumsq[...], axis=-1, keepdims=True) / model_width
+    root = lax.rsqrt(mean_square + epsilon)
+    gate = acc_g[...] * root
+    up = acc_u[...] * root
+    hid[...] = (gate * jax.nn.sigmoid(gate) * up).astype(jnp.bfloat16)
 
     for copy in down_copies:
         copy.wait()
@@ -273,24 +329,15 @@
     def column_of(k, parity):
         return pl.ds(pl.multiple_of((k * CORES + parity) * width, width), width)
 
-    def give(j, carry):
-        k = (far_chip + j) % pairs
-        share = jnp.dot(
-            hid[...], wd[:, column_of(k, 1 - core)], preferred_element_type=jnp.float32
-        )
+    def give(k):
+        share = jnp.dot(hid[...], wd[:, column_of(k, other)], preferred_element_type=jnp.float32)
         psend[k] = share.astype(jnp.bfloat16).reshape(groups, reqs, block_len, width)
         pair_copy(k).start()
-        return carry
-
-    def keep(j, carry):
-        k = (far_chip + j) % pairs
+
+    def keep(k):
         share = jnp.dot(hid[...], wd[:, column_of(k, core)], preferred_element_type=jnp.float32)
         pair_copy(k).wait_recv()
         csum[k] = share.reshape(groups, reqs, block_len, width) + precv[k].astype(jnp.float32)
-        return carry
-
-    lax.fori_loop(0, pairs, give, 0)
-    lax.fori_loop(0, pairs, keep, 0)
 
     def right_copy(t, i):
         return send(rsend.at[t, i], rrecv.at[t, i], r_ssem.at[t, i], r_rsem.at[t, i], right)
@@ -299,7 +346,8 @@
         return send(lsend.at[t, i], lrecv.at[t, i], l_ssem.at[t, i], l_rsem.at[t, i], left)
 
     sent = []
-    for t in range(half, 0, -1):
+
+    def ring_step(t):
         for i in range(reqs):
             for copy_of, out_buf, in_buf, offset, first in (
                 (right_copy, rsend, rrecv, t, goes_right(i)),
@@ -315,6 +363,27 @@
                 out_buf[t - 1, i] = value.astype(jnp.bfloat16)
                 copy_of(t - 1, i).start()
                 sent.append(copy_of(t - 1, i))
+
+    if paired:
+        give(k_far)
+        give(k_near)
+        keep(k_far)
+        ring_step(4)
+        give(k_next)
+        keep(k_near)
+        keep(k_next)
+        ring_step(3)
+        give(k_own)
+        keep(k_own)
+        ring_step(2)
+        ring_step(1)
+    else:
+        for j in range(pairs):
+            give(j)
+        for j in range(pairs):
+            keep(j)
+        for t in range(half, 0, -1):
+            ring_step(t)
     for i in range(reqs):
         right_copy(0, i).wait_recv()
         left_copy(0, i).wait_recv()
@@ -391,9 +460,9 @@
             pltpu.VMEM(w_up.shape, bf16),
             pltpu.VMEM(w_down.shape, bf16),
             pltpu.VMEM((count, reqs, block_len, width), bf16),
-            pltpu.VMEM((groups, rows, hidden_here), f32),
-            pltpu.VMEM((groups, rows, hidden_here), f32),
-            pltpu.VMEM((groups, rows, lanes), f32),
+            pltpu.VMEM((groups * rows, hidden_here), f32),
+            pltpu.VMEM((groups * rows, hidden_here), f32),
+            pltpu.VMEM((groups * rows, lanes), f32),
             pltpu.VMEM((groups * rows, hidden_here), bf16),
             pltpu.VMEM((pairs, groups, reqs, block_len, width), f32),
             pltpu.VMEM((pairs, groups, reqs, block_len, width), bf16),
@@ -416,7 +485,7 @@
             dma((half, reqs)),
         ],
         compiler_params=pltpu.CompilerParams(
-            collective_id=0, has_side_effects=True, vmem_limit_bytes=62 * 1024 * 1024
+            collective_id=0, has_side_effects=True, vmem_limit_bytes=57 * 1024 * 1024
         ),
         cost_estimate=pl.CostEstimate(
             flops=flops, bytes_accessed=6 * KVH * width * hidden_here, transcendentals=0

time: 60.5 us -> 58.6 us (0.969)
  Pallas kernels: 58.7 us -> 56.9 us
    pallas_call x1, Pallas kernels: 58.7 us -> 56.9 us  [body(): pl.pallas_call(functools.partial(layer_kernel, ring, snake), out_shape=ja...]
where the time goes in v2:
time: 58.6 us; the launch traced here: 58.5 us
  Pallas kernels  56.9 us (97%)
  local copies, waits for them, and re-layouts  1.57 us (3%)
    pallas_call x1, Pallas kernels, body(): pl.pallas_call(functools.partial(layer_kernel, ring, snake), out_shape=ja...  56.9 us
    unnamed x1, local copies, waits for them, and re-layouts  1.57 us

profile of v2, /device:TPU:0, one launch (start us, length us, event | category | flops | bytes accessed | tf_op | source)
XLA Modules:
  0.0 58.5 jit_solution(6663171556665579696)
XLA Ops:
  0.0 56.9 %shard_map.100 = bf16[2,32,1024]{2,1,0:T(8,128)(2,1)} custom-call(bf16[2,32,1024]{2,1,0:T(8,128)(2,1)} %bitcast.8, bf16[2,32,256]{2,1,0:T(8,128)(2,1)} %bitcast.10, bf16[2,1536,256]{2,1,0:T(8,128)(2,1)} %bitcast.6, s32[4]{0:T(128)} %prefix_ref.1, s32[4]{0:T(128)} %valid_ref.1, bf16[2,32,1024]{2,1,0:T(8,128)(2,1)} %bitcast.9, f32[1,8192]{1,0:T(1,128)} %bitcast.11, ...), custom_call_target="tpu_custom_call" | custom-call | flops 5637144576 | bytes 44040192 | tf_op jit(solution)/shard_map/pallas_call | solution.py:452
  56.9 1.6 %copy.12 = bf16[1,2,32,1024]{3,2,1,0:T(8,128)(2,1)} copy(bf16[1,2,32,1024]{3,2,1,0:T(8,128)(2,1)} %bitcast.7) | data formatting | bytes 262144

commit v3 on v2

--- a/solution.py
+++ b/solution.py
@@ -105,11 +105,11 @@
             barrier, inc=1, device_id={"ffn": other}, device_id_type=pl.DeviceIdType.MESH
         )
 
-    cache_copies = [
-        pltpu.make_async_copy(cache_hbm.at[r], cache.at[r], cache_sem.at[r]) for r in range(reqs)
-    ]
-    for copy in cache_copies:
-        copy.start()
+    def cache_copy(r):
+        return pltpu.make_async_copy(cache_hbm.at[r], cache.at[r], cache_sem.at[r])
+
+    for r in range(reqs):
+        cache_copy(r).start()
     weight_copies = []
     for w, (source, target) in enumerate(((wg_hbm, wg), (wu_hbm, wu))):
         for h in range(KVH):
@@ -150,11 +150,22 @@
 
     group = me // KVH
     scale = math.log2(math.e) / (head_size**0.5)
-    for r in range(reqs):
-        cache_copies[r].wait()
-        query = q_ref[r]
+    parts = 2 if heads % 2 == 0 else 1
+    part_heads = heads // parts
+    part_width = part_heads * head_size
+
+    def attend(step, carry):
+        r = step // parts
+        part = step % parts
+
+        @pl.when(part == 0)
+        def _():
+            cache_copy(r).wait()
+
+        columns = pl.ds(pl.multiple_of(part * part_width, part_width), part_width)
+        query = q_ref[r, :, columns]
         stacked = jnp.concatenate(
-            [query[:, h * head_size : (h + 1) * head_size] for h in range(heads)], axis=0
+            [query[:, h * head_size : (h + 1) * head_size] for h in range(part_heads)], axis=0
         )
         contract = (((1,), (1,)), ((), ()))
         far = lax.dot_general(
@@ -186,14 +197,24 @@
             preferred_element_type=jnp.float32,
         )
         side = jnp.concatenate(
-            [mixed[h * block_len : (h + 1) * block_len] for h in range(heads)], axis=1
-        )
-        xg[me, r] = (resid_ref[r].astype(jnp.float32) + side).astype(jnp.bfloat16)
-        if r == 0:
+            [mixed[h * block_len : (h + 1) * block_len] for h in range(part_heads)], axis=1
+        )
+        state = resid_ref[r, :, columns].astype(jnp.float32) + side
+        xg[me, r, :, columns] = state.astype(jnp.bfloat16)
+
+        @pl.when(step == parts - 1)
+        def _():
             pl.semaphore_wait(barrier, 3)
-        to_right(me, r).start()
-        to_left(me, r).start()
-        to_pair(me, r).start()
+
+        @pl.when(part == parts - 1)
+        def _():
+            to_right(me, r).start()
+            to_left(me, r).start()
+            to_pair(me, r).start()
+
+        return carry
+
+    lax.fori_loop(0, reqs * parts, attend, 0)
 
     def fold(square):
         folded = square[:, :head_size]
@@ -210,30 +231,15 @@
         acc_g[mine] += jnp.dot(scaled, wg[span, :], preferred_element_type=jnp.float32)
         acc_u[mine] += jnp.dot(scaled, wu[span, :], preferred_element_type=jnp.float32)
 
-    def absorb_heads(k, first=False):
-        span = pl.ds(pl.multiple_of(k * CORES * width, CORES * width), CORES * width)
+    def absorb_head(h):
+        span = pl.ds(pl.multiple_of(h * width, width), width)
         block = jnp.concatenate(
-            [
-                jnp.concatenate(
-                    [xg[g * KVH + k * CORES + c].reshape(rows, width) for c in range(CORES)],
-                    axis=1,
-                )
-                for g in range(groups)
-            ],
-            axis=0,
+            [xg[g * KVH + h].reshape(rows, width) for g in range(groups)], axis=0
         ).astype(jnp.float32)
-        squares = fold(block * block)
+        sumsq[...] += fold(block * block)
         scaled = (block * gain_ref[:, span]).astype(jnp.bfloat16)
-        gate = jnp.dot(scaled, wg[span, :], preferred_element_type=jnp.float32)
-        up = jnp.dot(scaled, wu[span, :], preferred_element_type=jnp.float32)
-        if first:
-            sumsq[...] = squares
-            acc_g[...] = gate
-            acc_u[...] = up
-        else:
-            sumsq[...] += squares
-            acc_g[...] += gate
-            acc_u[...] += up
+        acc_g[...] += jnp.dot(scaled, wg[span, :], preferred_element_type=jnp.float32)
+        acc_u[...] += jnp.dot(scaled, wu[span, :], preferred_element_type=jnp.float32)
 
     def pair_arrived(s):
         for i in range(reqs):
@@ -269,31 +275,51 @@
 
     far_chip = chip_at(half)
     other = 1 - core
-    k_own = chip % pairs
-    k_far = far_chip % pairs
+    acc_g[...] = jnp.zeros_like(acc_g)
+    acc_u[...] = jnp.zeros_like(acc_u)
+    sumsq[...] = jnp.zeros_like(sumsq)
+
+    def flipped(bits):
+        low = (chip + bits) % 2
+        high = (chip // 2 + bits // 2) % 2
+        return 2 * high + low
+
     if paired:
-        k_near = k_own + 1 - 2 * (k_own % 2)
-        k_next = pairs - 1 - k_near
-        pass_on(1, False)
-        pair_arrived(partner)
-        pass_on(2, False)
-        for t in (-1, 1, -2, 2):
+        def from_both(t):
+            pair_arrived(chip_at(-t) * CORES + other)
             pair_arrived(chip_at(t) * CORES + other)
-        for copy in weight_copies:
-            copy.wait()
-        absorb_heads(k_own, True)
-        pass_on(3, True)
-        for t in (-3, 3):
-            pair_arrived(chip_at(t) * CORES + other)
-        absorb_heads(k_near)
-        from_far()
-        absorb_heads(k_next)
-        pair_arrived(far_chip * CORES + other)
-        absorb_heads(k_far)
+
+        def stage(step, carry):
+            j = step // CORES
+
+            @pl.when(step == 0)
+            def _():
+                pass_on(1, False)
+                pair_arrived(partner)
+                pass_on(2, False)
+                from_both(1)
+                from_both(2)
+                for copy in weight_copies:
+                    copy.wait()
+
+            @pl.when(step == CORES)
+            def _():
+                pass_on(3, True)
+                from_both(3)
+
+            @pl.when(step == 2 * CORES)
+            def _():
+                from_far()
+
+            @pl.when(step == 3 * CORES)
+            def _():
+                pair_arrived(far_chip * CORES + other)
+
+            absorb_head(flipped(j) * CORES + step % CORES)
+            return carry
+
+        lax.fori_loop(0, KVH, stage, 0)
     else:
-        acc_g[...] = jnp.zeros_like(acc_g)
-        acc_u[...] = jnp.zeros_like(acc_u)
-        sumsq[...] = jnp.zeros_like(sumsq)
         pass_on(1, half == 2)
         for copy in weight_copies:
             copy.wait()
@@ -345,45 +371,76 @@
     def left_copy(t, i):
         return send(lsend.at[t, i], lrecv.at[t, i], l_ssem.at[t, i], l_rsem.at[t, i], left)
 
-    sent = []
+    def ring_move(t, i, first, copy_of, out_buf, in_buf, offset):
+        target = chip_at(offset)
+
+        def own():
+            return csum[target % pairs, target // pairs, i]
+
+        fed = (t < half - 1) | ((t == half - 1) & first)
+
+        @pl.when(fed)
+        def _():
+            copy_of(t, i).wait_recv()
+            total = own() + in_buf[t, i].astype(jnp.float32)
+            out_buf[t - 1, i] = total.astype(jnp.bfloat16)
+
+        @pl.when(jnp.logical_not(fed))
+        def _():
+            out_buf[t - 1, i] = own().astype(jnp.bfloat16)
+
+        copy_of(t - 1, i).start()
 
     def ring_step(t):
-        for i in range(reqs):
-            for copy_of, out_buf, in_buf, offset, first in (
-                (right_copy, rsend, rrecv, t, goes_right(i)),
-                (left_copy, lsend, lrecv, -t, not goes_right(i)),
-            ):
-                if t == half and not first:
-                    continue
-                target = chip_at(offset)
-                value = csum[target % pairs, target // pairs, i]
-                if t < half - 1 or (t == half - 1 and first):
-                    copy_of(t, i).wait_recv()
-                    value = value + in_buf[t, i].astype(jnp.float32)
-                out_buf[t - 1, i] = value.astype(jnp.bfloat16)
-                copy_of(t - 1, i).start()
-                sent.append(copy_of(t - 1, i))
+        def piece(i, carry):
+            first = i < reqs // 2
+
+            @pl.when((t < half) | first)
+            def _():
+                ring_move(t, i, first, right_copy, rsend, rrecv, t)
+
+            @pl.when((t < half) | jnp.logical_not(first))
+            def _():
+                ring_move(t, i, jnp.logical_not(first), left_copy, lsend, lrecv, -t)
+
+            return carry
+
+        lax.fori_loop(0, reqs, piece, 0)
 
     if paired:
-        give(k_far)
-        give(k_near)
-        keep(k_far)
-        ring_step(4)
-        give(k_next)
-        keep(k_near)
-        keep(k_next)
-        ring_step(3)
-        give(k_own)
-        keep(k_own)
-        ring_step(2)
-        ring_step(1)
+        def down(j, carry):
+            @pl.when(j < pairs)
+            def _():
+                give(flipped(pairs - 1 - j))
+
+            @pl.when((j > 0) & (j <= pairs))
+            def _():
+                keep(flipped(pairs - j))
+
+            @pl.when((j == 1) | (j > 2))
+            def _():
+                ring_step(jnp.minimum(half, half + 2 - j))
+
+            return carry
+
+        lax.fori_loop(0, pairs + 2, down, 0)
     else:
-        for j in range(pairs):
+
+        def give_one(j, carry):
             give(j)
-        for j in range(pairs):
+            return carry
+
+        def keep_one(j, carry):
             keep(j)
-        for t in range(half, 0, -1):
-            ring_step(t)
+            return carry
+
+        def ring_one(j, carry):
+            ring_step(half - j)
+            return carry
+
+        lax.fori_loop(0, pairs, give_one, 0)
+        lax.fori_loop(0, pairs, keep_one, 0)
+        lax.fori_loop(0, half, ring_one, 0)
     for i in range(reqs):
         right_copy(0, i).wait_recv()
         left_copy(0, i).wait_recv()
@@ -391,8 +448,15 @@
         value = value + rrecv[0, i].astype(jnp.float32) + lrecv[0, i].astype(jnp.float32)
         out_ref[i] = (xg[me, i].astype(jnp.float32) + value).astype(jnp.bfloat16)
 
-    for copy in sent:
-        copy.wait_send()
+    def ring_sent(t, carry):
+        for i in range(reqs):
+            right_copy(t, i).wait_send()
+            left_copy(t, i).wait_send()
+        return carry
+
+    lax.fori_loop(0, half - 1, ring_sent, 0)
+    for i in range(reqs):
+        (right_copy if goes_right(i) else left_copy)(half - 1, i).wait_send()
 
     def pair_sent(k, carry):
         pair_copy(k).wait_send()

time: 58.6 us -> 59.8 us (1.020)
  Pallas kernels: 56.9 us -> 58.1 us
    pallas_call x1, Pallas kernels: 56.9 us -> 58.1 us  [body(): pl.pallas_call(functools.partial(layer_kernel, ring, snake), out_shape=ja...]
where the time goes in v3:
time: 59.8 us; the launch traced here: 59.7 us
  Pallas kernels  58.1 us (97%)
  local copies, waits for them, and re-layouts  1.57 us (3%)
    pallas_call x1, Pallas kernels, body(): pl.pallas_call(functools.partial(layer_kernel, ring, snake), out_shape=ja...  58.1 us
    unnamed x1, local copies, waits for them, and re-layouts  1.57 us

profile of v3, /device:TPU:0, one launch (start us, length us, event | category | flops | bytes accessed | tf_op | source)
XLA Modules:
  0.0 59.7 jit_solution(5660340128771418147)
XLA Ops:
  0.0 58.1 %shard_map.100 = bf16[2,32,1024]{2,1,0:T(8,128)(2,1)} custom-call(bf16[2,32,1024]{2,1,0:T(8,128)(2,1)} %bitcast.8, bf16[2,32,256]{2,1,0:T(8,128)(2,1)} %bitcast.10, bf16[2,1536,256]{2,1,0:T(8,128)(2,1)} %bitcast.6, s32[4]{0:T(128)} %prefix_ref.1, s32[4]{0:T(128)} %valid_ref.1, bf16[2,32,1024]{2,1,0:T(8,128)(2,1)} %bitcast.9, f32[1,8192]{1,0:T(1,128)} %bitcast.11, ...), custom_call_target="tpu_custom_call" | custom-call | flops 5637144576 | bytes 44040192 | tf_op jit(solution)/shard_map/pallas_call | solution.py:516
  58.1 1.6 %copy.12 = bf16[1,2,32,1024]{3,2,1,0:T(8,128)(2,1)} copy(bf16[1,2,32,1024]{3,2,1,0:T(8,128)(2,1)} %bitcast.7) | data formatting | bytes 262144

commit v4 on v3

--- a/solution.py
+++ b/solution.py
@@ -110,21 +110,53 @@
 
     for r in range(reqs):
         cache_copy(r).start()
-    weight_copies = []
-    for w, (source, target) in enumerate(((wg_hbm, wg), (wu_hbm, wu))):
-        for h in range(KVH):
-            span = pl.ds(h * width, width)
-            weight_copies.append(
-                pltpu.make_async_copy(source.at[span], target.at[span], w_sem.at[w, h])
-            )
-    down_copies = []
-    for h in range(KVH):
-        span = pl.ds(h * width, width)
-        down_copies.append(
-            pltpu.make_async_copy(wd_hbm.at[:, span], wd.at[:, span], w_sem.at[2, h])
-        )
-    for copy in weight_copies + down_copies:
-        copy.start()
+
+    def flipped(bits):
+        low = (chip + bits) % 2
+        high = (chip // 2 + bits // 2) % 2
+        return 2 * high + low
+
+    far_chip = chip_at(half)
+    other = 1 - core
+
+    def gate_copy(h):
+        span = pl.ds(pl.multiple_of(h * width, width), width)
+        return pltpu.make_async_copy(wg_hbm.at[span], wg.at[span], w_sem.at[0, h])
+
+    def up_copy(h):
+        span = pl.ds(pl.multiple_of(h * width, width), width)
+        return pltpu.make_async_copy(wu_hbm.at[span], wu.at[span], w_sem.at[1, h])
+
+    def down_copy(h):
+        span = pl.ds(pl.multiple_of(h * width, width), width)
+        return pltpu.make_async_copy(wd_hbm.at[:, span], wd.at[:, span], w_sem.at[2, h])
+
+    def head_at(step):
+        return flipped(step // CORES) * CORES + step % CORES if paired else step
+
+    def start_gate_up(step, carry):
+        gate_copy(head_at(step)).start()
+        up_copy(head_at(step)).start()
+        return carry
+
+    def wait_gate_up(step, carry):
+        gate_copy(head_at(step)).wait()
+        up_copy(head_at(step)).wait()
+        return carry
+
+    def start_down(j, carry):
+        @pl.when(j < pairs)
+        def _():
+            down_copy(give_chip(j) * CORES + other).start()
+
+        @pl.when(j > 0)
+        def _():
+            down_copy(give_chip(j - 1) * CORES + core).start()
+
+        return carry
+
+    def give_chip(j):
+        return flipped(pairs - 1 - j) if paired else j
 
     def send(source, target, ssem, rsem, device):
         return pltpu.make_async_remote_copy(
@@ -158,9 +190,11 @@
         r = step // parts
         part = step % parts
 
-        @pl.when(part == 0)
+        @pl.when(step == 0)
         def _():
-            cache_copy(r).wait()
+            for i in range(reqs):
+                cache_copy(i).wait()
+            lax.fori_loop(0, KVH, start_gate_up, 0)
 
         columns = pl.ds(pl.multiple_of(part * part_width, part_width), part_width)
         query = q_ref[r, :, columns]
@@ -273,56 +307,42 @@
             (to_right if goes_right(i) else to_left)(far_chip * CORES + core, i).wait_recv()
             to_pair(far_chip * CORES + core, i).start()
 
-    far_chip = chip_at(half)
-    other = 1 - core
     acc_g[...] = jnp.zeros_like(acc_g)
     acc_u[...] = jnp.zeros_like(acc_u)
     sumsq[...] = jnp.zeros_like(sumsq)
-
-    def flipped(bits):
-        low = (chip + bits) % 2
-        high = (chip // 2 + bits // 2) % 2
-        return 2 * high + low
 
     if paired:
         def from_both(t):
             pair_arrived(chip_at(-t) * CORES + other)
             pair_arrived(chip_at(t) * CORES + other)
 
+        pass_on(1, False)
+        pair_arrived(partner)
+        pass_on(2, False)
+        lax.fori_loop(0, pairs + 1, start_down, 0)
+        from_both(1)
+        from_both(2)
+        pass_on(3, True)
+
         def stage(step, carry):
-            j = step // CORES
-
-            @pl.when(step == 0)
-            def _():
-                pass_on(1, False)
-                pair_arrived(partner)
-                pass_on(2, False)
-                from_both(1)
-                from_both(2)
-                for copy in weight_copies:
-                    copy.wait()
-
             @pl.when(step == CORES)
             def _():
-                pass_on(3, True)
                 from_both(3)
-
-            @pl.when(step == 2 * CORES)
-            def _():
                 from_far()
 
             @pl.when(step == 3 * CORES)
             def _():
                 pair_arrived(far_chip * CORES + other)
 
-            absorb_head(flipped(j) * CORES + step % CORES)
+            wait_gate_up(step, 0)
+            absorb_head(head_at(step))
             return carry
 
         lax.fori_loop(0, KVH, stage, 0)
     else:
         pass_on(1, half == 2)
-        for copy in weight_copies:
-            copy.wait()
+        lax.fori_loop(0, pairs + 1, start_down, 0)
+        lax.fori_loop(0, KVH, wait_gate_up, 0)
         absorb(me)
         absorb_pair(partner)
         absorb_step(1)
@@ -346,9 +366,6 @@
     up = acc_u[...] * root
     hid[...] = (gate * jax.nn.sigmoid(gate) * up).astype(jnp.bfloat16)
 
-    for copy in down_copies:
-        copy.wait()
-
     def pair_copy(k):
         return send(psend.at[k], precv.at[k], p_ssem.at[k], p_rsem.at[k], partner)
 
@@ -356,11 +373,13 @@
         return pl.ds(pl.multiple_of((k * CORES + parity) * width, width), width)
 
     def give(k):
+        down_copy(k * CORES + other).wait()
         share = jnp.dot(hid[...], wd[:, column_of(k, other)], preferred_element_type=jnp.float32)
         psend[k] = share.astype(jnp.bfloat16).reshape(groups, reqs, block_len, width)
         pair_copy(k).start()
 
     def keep(k):
+        down_copy(k * CORES + core).wait()
         share = jnp.dot(hid[...], wd[:, column_of(k, core)], preferred_element_type=jnp.float32)
         pair_copy(k).wait_recv()
         csum[k] = share.reshape(groups, reqs, block_len, width) + precv[k].astype(jnp.float32)
@@ -411,11 +430,11 @@
         def down(j, carry):
             @pl.when(j < pairs)
             def _():
-                give(flipped(pairs - 1 - j))
+                give(give_chip(j))
 
             @pl.when((j > 0) & (j <= pairs))
             def _():
-                keep(flipped(pairs - j))
+                keep(give_chip(j - 1))
 
             @pl.when((j == 1) | (j > 2))
             def _():

time: 59.8 us -> 50.5 us (0.84)
  Pallas kernels: 58.1 us -> 48.8 us
    pallas_call x1, Pallas kernels: 58.1 us -> 48.8 us  [body(): pl.pallas_call(functools.partial(layer_kernel, ring, snake), out_shape=ja...]
where the time goes in v4:
time: 50.5 us; the launch traced here: 50.4 us
  Pallas kernels  48.8 us (97%)
  local copies, waits for them, and re-layouts  1.57 us (3%)
    pallas_call x1, Pallas kernels, body(): pl.pallas_call(functools.partial(layer_kernel, ring, snake), out_shape=ja...  48.8 us
    unnamed x1, local copies, waits for them, and re-layouts  1.57 us

profile of v4, /device:TPU:0, one launch (start us, length us, event | category | flops | bytes accessed | tf_op | source)
XLA Modules:
  0.0 50.4 jit_solution(8952776631772695760)
XLA Ops:
  0.0 48.8 %shard_map.100 = bf16[2,32,1024]{2,1,0:T(8,128)(2,1)} custom-call(bf16[2,32,1024]{2,1,0:T(8,128)(2,1)} %bitcast.8, bf16[2,32,256]{2,1,0:T(8,128)(2,1)} %bitcast.10, bf16[2,1536,256]{2,1,0:T(8,128)(2,1)} %bitcast.6, s32[4]{0:T(128)} %prefix_ref.1, s32[4]{0:T(128)} %valid_ref.1, bf16[2,32,1024]{2,1,0:T(8,128)(2,1)} %bitcast.9, f32[1,8192]{1,0:T(1,128)} %bitcast.11, ...), custom_call_target="tpu_custom_call" | custom-call | flops 5637144576 | bytes 44040192 | tf_op jit(solution)/shard_map/pallas_call | solution.py:535
  48.8 1.6 %copy.12 = bf16[1,2,32,1024]{3,2,1,0:T(8,128)(2,1)} copy(bf16[1,2,32,1024]{3,2,1,0:T(8,128)(2,1)} %bitcast.7) | data formatting | bytes 262144

commit v5 on v4

--- a/solution.py
+++ b/solution.py
@@ -77,6 +77,8 @@
     model_width = KVH * width
     rows = reqs * block_len
     groups = acc_g.shape[0] // rows
+    pieces, piece_len = xg.shape[1:3]
+    splits = pieces // reqs
     pairs = KVH // CORES
     half = ring // 2
     paired = snake and ring == 2 * pairs == 8 and groups == 2
@@ -178,7 +180,7 @@
         return send(xg.at[s, i], xg.at[s, i], ag_pair.at[s, i], ag_recv.at[s, i], partner)
 
     def goes_right(i):
-        return i < reqs // 2
+        return i < pieces // 2
 
     group = me // KVH
     scale = math.log2(math.e) / (head_size**0.5)
@@ -234,7 +236,10 @@
             [mixed[h * block_len : (h + 1) * block_len] for h in range(part_heads)], axis=1
         )
         state = resid_ref[r, :, columns].astype(jnp.float32) + side
-        xg[me, r, :, columns] = state.astype(jnp.bfloat16)
+        for piece in range(splits):
+            xg[me, r * splits + piece, :, columns] = state[
+                piece * piece_len : (piece + 1) * piece_len
+            ].astype(jnp.bfloat16)
 
         @pl.when(step == parts - 1)
         def _():
@@ -242,9 +247,11 @@
 
         @pl.when(part == parts - 1)
         def _():
-            to_right(me, r).start()
-            to_left(me, r).start()
-            to_pair(me, r).start()
+            for piece in range(splits):
+                i = r * splits + piece
+                to_right(me, i).start()
+                to_left(me, i).start()
+                to_pair(me, i).start()
 
         return carry
 
@@ -276,7 +283,7 @@
         acc_u[...] += jnp.dot(scaled, wu[span, :], preferred_element_type=jnp.float32)
 
     def pair_arrived(s):
-        for i in range(reqs):
+        for i in range(pieces):
             to_pair(s, i).wait_recv()
 
     def absorb_pair(s):
@@ -286,7 +293,7 @@
     def pass_on(t, last):
         from_left = chip_at(-t) * CORES + core
         from_right = chip_at(t) * CORES + core
-        for i in range(reqs):
+        for i in range(pieces):
             to_right(from_left, i).wait_recv()
             if not last or goes_right(i):
                 to_right(from_left, i).start()
@@ -303,7 +310,7 @@
         absorb_pair(chip_at(t) * CORES + 1 - core)
 
     def from_far():
-        for i in range(reqs):
+        for i in range(pieces):
             (to_right if goes_right(i) else to_left)(far_chip * CORES + core, i).wait_recv()
             to_pair(far_chip * CORES + core, i).start()
 
@@ -322,12 +329,18 @@
         lax.fori_loop(0, pairs + 1, start_down, 0)
         from_both(1)
         from_both(2)
-        pass_on(3, True)
 
         def stage(step, carry):
+            @pl.when(step == 1)
+            def _():
+                pass_on(3, True)
+
             @pl.when(step == CORES)
             def _():
                 from_both(3)
+
+            @pl.when(step == CORES + 1)
+            def _():
                 from_far()
 
             @pl.when(step == 3 * CORES)
@@ -375,14 +388,14 @@
     def give(k):
         down_copy(k * CORES + other).wait()
         share = jnp.dot(hid[...], wd[:, column_of(k, other)], preferred_element_type=jnp.float32)
-        psend[k] = share.astype(jnp.bfloat16).reshape(groups, reqs, block_len, width)
+        psend[k] = share.astype(jnp.bfloat16).reshape(groups, pieces, piece_len, width)
         pair_copy(k).start()
 
     def keep(k):
         down_copy(k * CORES + core).wait()
         share = jnp.dot(hid[...], wd[:, column_of(k, core)], preferred_element_type=jnp.float32)
         pair_copy(k).wait_recv()
-        csum[k] = share.reshape(groups, reqs, block_len, width) + precv[k].astype(jnp.float32)
+        csum[k] = share.reshape(groups, pieces, piece_len, width) + precv[k].astype(jnp.float32)
 
     def right_copy(t, i):
         return send(rsend.at[t, i], rrecv.at[t, i], r_ssem.at[t, i], r_rsem.at[t, i], right)
@@ -412,19 +425,16 @@
 
     def ring_step(t):
         def piece(i, carry):
-            first = i < reqs // 2
-
-            @pl.when((t < half) | first)
-            def _():
-                ring_move(t, i, first, right_copy, rsend, rrecv, t)
-
-            @pl.when((t < half) | jnp.logical_not(first))
-            def _():
-                ring_move(t, i, jnp.logical_not(first), left_copy, lsend, lrecv, -t)
+            late = i >= pieces // 2
+
+            @pl.when((t < half) | late)
+            def _():
+                ring_move(t, pieces - 1 - i, late, right_copy, rsend, rrecv, t)
+                ring_move(t, i, late, left_copy, lsend, lrecv, -t)
 
             return carry
 
-        lax.fori_loop(0, reqs, piece, 0)
+        lax.fori_loop(0, pieces, piece, 0)
 
     if paired:
         def down(j, carry):
@@ -460,21 +470,22 @@
         lax.fori_loop(0, pairs, give_one, 0)
         lax.fori_loop(0, pairs, keep_one, 0)
         lax.fori_loop(0, half, ring_one, 0)
-    for i in range(reqs):
+    for i in range(pieces):
         right_copy(0, i).wait_recv()
         left_copy(0, i).wait_recv()
         value = csum[chip % pairs, chip // pairs, i]
         value = value + rrecv[0, i].astype(jnp.float32) + lrecv[0, i].astype(jnp.float32)
-        out_ref[i] = (xg[me, i].astype(jnp.float32) + value).astype(jnp.bfloat16)
+        within = pl.ds(i % splits * piece_len, piece_len)
+        out_ref[i // splits, within] = (xg[me, i].astype(jnp.float32) + value).astype(jnp.bfloat16)
 
     def ring_sent(t, carry):
-        for i in range(reqs):
+        for i in range(pieces):
             right_copy(t, i).wait_send()
             left_copy(t, i).wait_send()
         return carry
 
     lax.fori_loop(0, half - 1, ring_sent, 0)
-    for i in range(reqs):
+    for i in range(pieces):
         (right_copy if goes_right(i) else left_copy)(half - 1, i).wait_send()
 
     def pair_sent(k, carry):
@@ -484,14 +495,14 @@
     lax.fori_loop(0, pairs, pair_sent, 0)
 
     def gather_sent(t, carry):
-        for i in range(reqs):
+        for i in range(pieces):
             to_right(chip_at(-t) * CORES + core, i).wait_send()
             to_pair(chip_at(-t) * CORES + core, i).wait_send()
             to_left(chip_at(t) * CORES + core, i).wait_send()
             to_pair(chip_at(t) * CORES + core, i).wait_send()
         return carry
 
-    for i in range(reqs):
+    for i in range(pieces):
         to_right(me, i).wait_send()
         to_left(me, i).wait_send()
         to_pair(me, i).wait_send()
@@ -526,6 +537,8 @@
     rows = reqs * block_len
     pairs = KVH // CORES
     lanes = block_kv.shape[3] // 2
+    splits = 2 if block_len % 32 == 0 else 1
+    pieces, piece_len = reqs * splits, block_len // splits
     bf16, f32 = jnp.bfloat16, jnp.float32
     vmem = pl.BlockSpec(memory_space=pltpu.VMEM)
     smem = pl.BlockSpec(memory_space=pltpu.SMEM)
@@ -542,30 +555,30 @@
             pltpu.VMEM(w_gate.shape, bf16),
             pltpu.VMEM(w_up.shape, bf16),
             pltpu.VMEM(w_down.shape, bf16),
-            pltpu.VMEM((count, reqs, block_len, width), bf16),
+            pltpu.VMEM((count, pieces, piece_len, width), bf16),
             pltpu.VMEM((groups * rows, hidden_here), f32),
             pltpu.VMEM((groups * rows, hidden_here), f32),
             pltpu.VMEM((groups * rows, lanes), f32),
             pltpu.VMEM((groups * rows, hidden_here), bf16),
-            pltpu.VMEM((pairs, groups, reqs, block_len, width), f32),
-            pltpu.VMEM((pairs, groups, reqs, block_len, width), bf16),
-            pltpu.VMEM((pairs, groups, reqs, block_len, width), bf16),
-            pltpu.VMEM((half, reqs, block_len, width), bf16),
-            pltpu.VMEM((half, reqs, block_len, width), bf16),
-            pltpu.VMEM((half, reqs, block_len, width), bf16),
-            pltpu.VMEM((half, reqs, block_len, width), bf16),
+            pltpu.VMEM((pairs, groups, pieces, piece_len, width), f32),
+            pltpu.VMEM((pairs, groups, pieces, piece_len, width), bf16),
+            pltpu.VMEM((pairs, groups, pieces, piece_len, width), bf16),
+            pltpu.VMEM((half, pieces, piece_len, width), bf16),
+            pltpu.VMEM((half, pieces, piece_len, width), bf16),
+            pltpu.VMEM((half, pieces, piece_len, width), bf16),
+            pltpu.VMEM((half, pieces, piece_len, width), bf16),
             dma((reqs,)),
             dma((3, KVH)),
-            dma((count, reqs)),
-            dma((count, reqs)),
-            dma((count, reqs)),
-            dma((count, reqs)),
+            dma((count, pieces)),
+            dma((count, pieces)),
+            dma((count, pieces)),
+            dma((count, pieces)),
             dma((pairs,)),
             dma((pairs,)),
-            dma((half, reqs)),
-            dma((half, reqs)),
-            dma((half, reqs)),
-            dma((half, reqs)),
+            dma((half, pieces)),
+            dma((half, pieces)),
+            dma((half, pieces)),
+            dma((half, pieces)),
         ],
         compiler_params=pltpu.CompilerParams(
             collective_id=0, has_side_effects=True, vmem_limit_bytes=57 * 1024 * 1024

time: 50.5 us -> 47.5 us (0.941)
  Pallas kernels: 48.8 us -> 45.8 us
    pallas_call x1, Pallas kernels: 48.8 us -> 45.8 us  [body(): pl.pallas_call(functools.partial(layer_kernel, ring, snake), out_shape=ja...]
where the time goes in v5:
time: 47.5 us; the launch traced here: 47.4 us
  Pallas kernels  45.8 us (96%)
  local copies, waits for them, and re-layouts  1.57 us (3%)
    pallas_call x1, Pallas kernels, body(): pl.pallas_call(functools.partial(layer_kernel, ring, snake), out_shape=ja...  45.8 us
    unnamed x1, local copies, waits for them, and re-layouts  1.57 us

profile of v5, /device:TPU:0, one launch (start us, length us, event | category | flops | bytes accessed | tf_op | source)
XLA Modules:
  0.0 47.4 jit_solution(9498070240164404471)
XLA Ops:
  0.0 45.8 %shard_map.100 = bf16[2,32,1024]{2,1,0:T(8,128)(2,1)} custom-call(bf16[2,32,1024]{2,1,0:T(8,128)(2,1)} %bitcast.8, bf16[2,32,256]{2,1,0:T(8,128)(2,1)} %bitcast.10, bf16[2,1536,256]{2,1,0:T(8,128)(2,1)} %bitcast.6, s32[4]{0:T(128)} %prefix_ref.1, s32[4]{0:T(128)} %valid_ref.1, bf16[2,32,1024]{2,1,0:T(8,128)(2,1)} %bitcast.9, f32[1,8192]{1,0:T(1,128)} %bitcast.11, ...), custom_call_target="tpu_custom_call" | custom-call | flops 5637144576 | bytes 44040192 | tf_op jit(solution)/shard_map/pallas_call | solution.py:548
  45.8 1.6 %copy.12 = bf16[1,2,32,1024]{3,2,1,0:T(8,128)(2,1)} copy(bf16[1,2,32,1024]{3,2,1,0:T(8,128)(2,1)} %bitcast.7) | data formatting | bytes 262144

commit v6 on v5

--- a/solution.py
+++ b/solution.py
@@ -29,17 +29,21 @@
 def layer_kernel(
     ring,
     snake,
-    q_ref,
-    bkv_ref,
+    q_hbm,
+    bkv_hbm,
     cache_hbm,
     prefix_ref,
     valid_ref,
-    resid_ref,
-    gain_ref,
+    resid_hbm,
+    gain_hbm,
     wg_hbm,
     wu_hbm,
     wd_hbm,
     out_ref,
+    q_ref,
+    bkv_ref,
+    resid_ref,
+    gain_ref,
     cache,
     wg,
     wu,
@@ -56,12 +60,14 @@
     rrecv,
     lsend,
     lrecv,
+    in_sem,
     cache_sem,
     w_sem,
     ag_recv,
     ag_right,
     ag_left,
     ag_pair,
+    ag_pair_recv,
     p_ssem,
     p_rsem,
     r_ssem,
@@ -77,8 +83,10 @@
     model_width = KVH * width
     rows = reqs * block_len
     groups = acc_g.shape[0] // rows
-    pieces, piece_len = xg.shape[1:3]
-    splits = pieces // reqs
+    pieces = xg.shape[1]
+    part_width = xg.shape[3]
+    parts = pieces // reqs
+    part_heads = part_width // head_size
     pairs = KVH // CORES
     half = ring // 2
     paired = snake and ring == 2 * pairs == 8 and groups == 2
@@ -110,6 +118,14 @@
     def cache_copy(r):
         return pltpu.make_async_copy(cache_hbm.at[r], cache.at[r], cache_sem.at[r])
 
+    small_copies = [
+        pltpu.make_async_copy(source, target, in_sem.at[n])
+        for n, (source, target) in enumerate(
+            ((q_hbm, q_ref), (bkv_hbm, bkv_ref), (resid_hbm, resid_ref), (gain_hbm, gain_ref))
+        )
+    ]
+    for copy in small_copies:
+        copy.start()
     for r in range(reqs):
         cache_copy(r).start()
 
@@ -176,27 +192,23 @@
     def to_left(s, i):
         return send(xg.at[s, i], xg.at[s, i], ag_left.at[s, i], ag_recv.at[s, i], left)
 
-    def to_pair(s, i):
-        return send(xg.at[s, i], xg.at[s, i], ag_pair.at[s, i], ag_recv.at[s, i], partner)
+    def to_pair(s):
+        return send(xg.at[s], xg.at[s], ag_pair.at[s], ag_pair_recv.at[s], partner)
 
     def goes_right(i):
         return i < pieces // 2
 
     group = me // KVH
     scale = math.log2(math.e) / (head_size**0.5)
-    parts = 2 if heads % 2 == 0 else 1
-    part_heads = heads // parts
-    part_width = part_heads * head_size
+    for copy in small_copies:
+        copy.wait()
+    for r in range(reqs):
+        cache_copy(r).wait()
+    lax.fori_loop(0, KVH, start_gate_up, 0)
 
     def attend(step, carry):
         r = step // parts
         part = step % parts
-
-        @pl.when(step == 0)
-        def _():
-            for i in range(reqs):
-                cache_copy(i).wait()
-            lax.fori_loop(0, KVH, start_gate_up, 0)
 
         columns = pl.ds(pl.multiple_of(part * part_width, part_width), part_width)
         query = q_ref[r, :, columns]
@@ -236,26 +248,27 @@
             [mixed[h * block_len : (h + 1) * block_len] for h in range(part_heads)], axis=1
         )
         state = resid_ref[r, :, columns].astype(jnp.float32) + side
-        for piece in range(splits):
-            xg[me, r * splits + piece, :, columns] = state[
-                piece * piece_len : (piece + 1) * piece_len
-            ].astype(jnp.bfloat16)
-
-        @pl.when(step == parts - 1)
+        xg[me, step] = state.astype(jnp.bfloat16)
+
+        @pl.when(step == 0)
         def _():
             pl.semaphore_wait(barrier, 3)
 
-        @pl.when(part == parts - 1)
-        def _():
-            for piece in range(splits):
-                i = r * splits + piece
-                to_right(me, i).start()
-                to_left(me, i).start()
-                to_pair(me, i).start()
-
+        to_right(me, step).start()
+        to_left(me, step).start()
         return carry
 
-    lax.fori_loop(0, reqs * parts, attend, 0)
+    lax.fori_loop(0, pieces, attend, 0)
+    to_pair(me).start()
+
+    def block_of(s):
+        return jnp.concatenate(
+            [
+                jnp.concatenate([xg[s, r * parts + part] for part in range(parts)], axis=1)
+                for r in range(reqs)
+            ],
+            axis=0,
+        )
 
     def fold(square):
         folded = square[:, :head_size]
@@ -266,7 +279,7 @@
     def absorb(s):
         mine = pl.ds(pl.multiple_of((s // KVH) * rows, rows), rows)
         span = pl.ds(pl.multiple_of((s % KVH) * width, width), width)
-        block = xg[s].reshape(rows, width).astype(jnp.float32)
+        block = block_of(s).astype(jnp.float32)
         sumsq[mine] += fold(block * block)
         scaled = (block * gain_ref[:, span]).astype(jnp.bfloat16)
         acc_g[mine] += jnp.dot(scaled, wg[span, :], preferred_element_type=jnp.float32)
@@ -275,7 +288,7 @@
     def absorb_head(h):
         span = pl.ds(pl.multiple_of(h * width, width), width)
         block = jnp.concatenate(
-            [xg[g * KVH + h].reshape(rows, width) for g in range(groups)], axis=0
+            [block_of(g * KVH + h) for g in range(groups)], axis=0
         ).astype(jnp.float32)
         sumsq[...] += fold(block * block)
         scaled = (block * gain_ref[:, span]).astype(jnp.bfloat16)
@@ -283,8 +296,7 @@
         acc_u[...] += jnp.dot(scaled, wu[span, :], preferred_element_type=jnp.float32)
 
     def pair_arrived(s):
-        for i in range(pieces):
-            to_pair(s, i).wait_recv()
+        to_pair(s).wait_recv()
 
     def absorb_pair(s):
         pair_arrived(s)
@@ -297,11 +309,11 @@
             to_right(from_left, i).wait_recv()
             if not last or goes_right(i):
                 to_right(from_left, i).start()
-            to_pair(from_left, i).start()
             to_left(from_right, i).wait_recv()
             if not last or not goes_right(i):
                 to_left(from_right, i).start()
-            to_pair(from_right, i).start()
+        to_pair(from_left).start()
+        to_pair(from_right).start()
 
     def absorb_step(t):
         absorb(chip_at(-t) * CORES + core)
@@ -312,7 +324,7 @@
     def from_far():
         for i in range(pieces):
             (to_right if goes_right(i) else to_left)(far_chip * CORES + core, i).wait_recv()
-            to_pair(far_chip * CORES + core, i).start()
+        to_pair(far_chip * CORES + core).start()
 
     acc_g[...] = jnp.zeros_like(acc_g)
     acc_u[...] = jnp.zeros_like(acc_u)
@@ -385,17 +397,26 @@
     def column_of(k, parity):
         return pl.ds(pl.multiple_of((k * CORES + parity) * width, width), width)
 
+    cuts = []
+    for g in range(groups):
+        for i in range(pieces):
+            top = g * rows + i // parts * block_len
+            side = i % parts * part_width
+            cuts.append((g, i, (slice(top, top + block_len), slice(side, side + part_width))))
+
     def give(k):
         down_copy(k * CORES + other).wait()
         share = jnp.dot(hid[...], wd[:, column_of(k, other)], preferred_element_type=jnp.float32)
-        psend[k] = share.astype(jnp.bfloat16).reshape(groups, pieces, piece_len, width)
+        for g, i, cut in cuts:
+            psend[k, g, i] = share[cut].astype(jnp.bfloat16)
         pair_copy(k).start()
 
     def keep(k):
         down_copy(k * CORES + core).wait()
         share = jnp.dot(hid[...], wd[:, column_of(k, core)], preferred_element_type=jnp.float32)
         pair_copy(k).wait_recv()
-        csum[k] = share.reshape(groups, pieces, piece_len, width) + precv[k].astype(jnp.float32)
+        for g, i, cut in cuts:
+            csum[k, g, i] = share[cut] + precv[k, g, i].astype(jnp.float32)
 
     def right_copy(t, i):
         return send(rsend.at[t, i], rrecv.at[t, i], r_ssem.at[t, i], r_rsem.at[t, i], right)
@@ -475,8 +496,9 @@
         left_copy(0, i).wait_recv()
         value = csum[chip % pairs, chip // pairs, i]
         value = value + rrecv[0, i].astype(jnp.float32) + lrecv[0, i].astype(jnp.float32)
-        within = pl.ds(i % splits * piece_len, piece_len)
-        out_ref[i // splits, within] = (xg[me, i].astype(jnp.float32) + value).astype(jnp.bfloat16)
+        columns = pl.ds(i % parts * part_width, part_width)
+        value = xg[me, i].astype(jnp.float32) + value
+        out_ref[i // parts, :, columns] = value.astype(jnp.bfloat16)
 
     def ring_sent(t, carry):
         for i in range(pieces):
@@ -497,21 +519,20 @@
     def gather_sent(t, carry):
         for i in range(pieces):
             to_right(chip_at(-t) * CORES + core, i).wait_send()
-            to_pair(chip_at(-t) * CORES + core, i).wait_send()
             to_left(chip_at(t) * CORES + core, i).wait_send()
-            to_pair(chip_at(t) * CORES + core, i).wait_send()
+        to_pair(chip_at(-t) * CORES + core).wait_send()
+        to_pair(chip_at(t) * CORES + core).wait_send()
         return carry
 
     for i in range(pieces):
         to_right(me, i).wait_send()
         to_left(me, i).wait_send()
-        to_pair(me, i).wait_send()
-        to_pair(far_chip * CORES + core, i).wait_send()
-        (to_right(chip_at(1 - half) * CORES + core, i) if goes_right(i) else to_left(
-            chip_at(half - 1) * CORES + core, i
-        )).wait_send()
-        to_pair(chip_at(1 - half) * CORES + core, i).wait_send()
-        to_pair(chip_at(half - 1) * CORES + core, i).wait_send()
+        if goes_right(i):
+            to_right(chip_at(1 - half) * CORES + core, i).wait_send()
+        else:
+            to_left(chip_at(half - 1) * CORES + core, i).wait_send()
+    for s in (me, *(chip_at(t) * CORES + core for t in (half, half - 1, 1 - half))):
+        to_pair(s).wait_send()
     lax.fori_loop(1, half - 1, gather_sent, 0)
 
 
@@ -537,8 +558,8 @@
     rows = reqs * block_len
     pairs = KVH // CORES
     lanes = block_kv.shape[3] // 2
-    splits = 2 if block_len % 32 == 0 else 1
-    pieces, piece_len = reqs * splits, block_len // splits
+    parts = 2 if (width // lanes) % 2 == 0 else 1
+    pieces, part_width = reqs * parts, width // parts
     bf16, f32 = jnp.bfloat16, jnp.float32
     vmem = pl.BlockSpec(memory_space=pltpu.VMEM)
     smem = pl.BlockSpec(memory_space=pltpu.SMEM)
@@ -548,31 +569,37 @@
     out = pl.pallas_call(
         functools.partial(layer_kernel, ring, snake),
         out_shape=jax.ShapeDtypeStruct((reqs, block_len, width), bf16),
-        in_specs=[vmem, vmem, hbm, smem, smem, vmem, vmem, hbm, hbm, hbm],
+        in_specs=[hbm, hbm, hbm, smem, smem, hbm, hbm, hbm, hbm, hbm],
         out_specs=vmem,
         scratch_shapes=[
+            pltpu.VMEM(queries.shape[1:], bf16),
+            pltpu.VMEM(block_kv.shape[1:], bf16),
+            pltpu.VMEM(resid.shape[1:], bf16),
+            pltpu.VMEM((1, norm_gain.shape[0]), f32),
             pltpu.VMEM(cache_kv.shape[1:], bf16),
             pltpu.VMEM(w_gate.shape, bf16),
             pltpu.VMEM(w_up.shape, bf16),
             pltpu.VMEM(w_down.shape, bf16),
-            pltpu.VMEM((count, pieces, piece_len, width), bf16),
+            pltpu.VMEM((count, pieces, block_len, part_width), bf16),
             pltpu.VMEM((groups * rows, hidden_here), f32),
             pltpu.VMEM((groups * rows, hidden_here), f32),
             pltpu.VMEM((groups * rows, lanes), f32),
             pltpu.VMEM((groups * rows, hidden_here), bf16),
-            pltpu.VMEM((pairs, groups, pieces, piece_len, width), f32),
-            pltpu.VMEM((pairs, groups, pieces, piece_len, width), bf16),
-            pltpu.VMEM((pairs, groups, pieces, piece_len, width), bf16),
-            pltpu.VMEM((half, pieces, piece_len, width), bf16),
-            pltpu.VMEM((half, pieces, piece_len, width), bf16),
-            pltpu.VMEM((half, pieces, piece_len, width), bf16),
-            pltpu.VMEM((half, pieces, piece_len, width), bf16),
+            pltpu.VMEM((pairs, groups, pieces, block_len, part_width), f32),
+            pltpu.VMEM((pairs, groups, pieces, block_len, part_width), bf16),
+            pltpu.VMEM((pairs, groups, pieces, block_len, part_width), bf16),
+            pltpu.VMEM((half, pieces, block_len, part_width), bf16),
+            pltpu.VMEM((half, pieces, block_len, part_width), bf16),
+            pltpu.VMEM((half, pieces, block_len, part_width), bf16),
+            pltpu.VMEM((half, pieces, block_len, part_width), bf16),
+            dma((4,)),
             dma((reqs,)),
             dma((3, KVH)),
             dma((count, pieces)),
             dma((count, pieces)),
             dma((count, pieces)),
-            dma((count, pieces)),
+            dma((count,)),
+            dma((count,)),
             dma((pairs,)),
             dma((pairs,)),
             dma((half, pieces)),

time: 47.5 us -> 46.2 us (0.973)
  Pallas kernels: 45.8 us -> 44.5 us
    pallas_call x1, Pallas kernels: 45.8 us -> 44.5 us  [body(): pl.pallas_call(functools.partial(layer_kernel, ring, snake), out_shape=ja...]
where the time goes in v6:
time: 46.2 us; the launch traced here: 46 us
  Pallas kernels  44.5 us (96%)
  local copies, waits for them, and re-layouts  1.57 us (3%)
    pallas_call x1, Pallas kernels, body(): pl.pallas_call(functools.partial(layer_kernel, ring, snake), out_shape=ja...  44.5 us
    unnamed x1, local copies, waits for them, and re-layouts  1.57 us

profile of v6, /device:TPU:0, one launch (start us, length us, event | category | flops | bytes accessed | tf_op | source)
XLA Modules:
  0.0 46.0 jit_solution(12712174519294088862)
XLA Ops:
  0.0 44.5 %shard_map.100 = bf16[2,32,1024]{2,1,0:T(8,128)(2,1)} custom-call(bf16[2,32,1024]{2,1,0:T(8,128)(2,1)} %bitcast.8, bf16[2,32,256]{2,1,0:T(8,128)(2,1)} %bitcast.10, bf16[2,1536,256]{2,1,0:T(8,128)(2,1)} %bitcast.6, s32[4]{0:T(128)} %prefix_ref.1, s32[4]{0:T(128)} %valid_ref.1, bf16[2,32,1024]{2,1,0:T(8,128)(2,1)} %bitcast.9, f32[1,8192]{1,0:T(1,128)} %bitcast.11, ...), custom_call_target="tpu_custom_call" | custom-call | flops 5637144576 | bytes 44040192 | tf_op jit(solution)/shard_map/pallas_call | solution.py:569
  44.5 1.6 %copy.12 = bf16[1,2,32,1024]{3,2,1,0:T(8,128)(2,1)} copy(bf16[1,2,32,1024]{3,2,1,0:T(8,128)(2,1)} %bitcast.7) | data formatting | bytes 262144

commit v7 on v6

--- a/solution.py
+++ b/solution.py
@@ -285,10 +285,16 @@
         acc_g[mine] += jnp.dot(scaled, wg[span, :], preferred_element_type=jnp.float32)
         acc_u[mine] += jnp.dot(scaled, wu[span, :], preferred_element_type=jnp.float32)
 
-    def absorb_head(h):
-        span = pl.ds(pl.multiple_of(h * width, width), width)
+    def absorb_heads(k):
+        span = pl.ds(pl.multiple_of(k * CORES * width, CORES * width), CORES * width)
         block = jnp.concatenate(
-            [block_of(g * KVH + h) for g in range(groups)], axis=0
+            [
+                jnp.concatenate(
+                    [block_of(g * KVH + k * CORES + c) for c in range(CORES)], axis=1
+                )
+                for g in range(groups)
+            ],
+            axis=0,
         ).astype(jnp.float32)
         sumsq[...] += fold(block * block)
         scaled = (block * gain_ref[:, span]).astype(jnp.bfloat16)
@@ -342,28 +348,26 @@
         from_both(1)
         from_both(2)
 
-        def stage(step, carry):
-            @pl.when(step == 1)
+        def stage(j, carry):
+            @pl.when(j == 1)
             def _():
                 pass_on(3, True)
-
-            @pl.when(step == CORES)
-            def _():
                 from_both(3)
 
-            @pl.when(step == CORES + 1)
+            @pl.when(j == 2)
             def _():
                 from_far()
 
-            @pl.when(step == 3 * CORES)
+            @pl.when(j == 3)
             def _():
                 pair_arrived(far_chip * CORES + other)
 
-            wait_gate_up(step, 0)
-            absorb_head(head_at(step))
+            for c in range(CORES):
+                wait_gate_up(j * CORES + c, 0)
+            absorb_heads(flipped(j))
             return carry
 
-        lax.fori_loop(0, KVH, stage, 0)
+        lax.fori_loop(0, pairs, stage, 0)
     else:
         pass_on(1, half == 2)
         lax.fori_loop(0, pairs + 1, start_down, 0)

time: 46.2 us -> 45 us (0.974)
  Pallas kernels: 44.5 us -> 43.3 us
    pallas_call x1, Pallas kernels: 44.5 us -> 43.3 us  [body(): pl.pallas_call(functools.partial(layer_kernel, ring, snake), out_shape=ja...]
where the time goes in v7:
time: 45 us; the launch traced here: 44.9 us
  Pallas kernels  43.3 us (96%)
  local copies, waits for them, and re-layouts  1.57 us (3%)
    pallas_call x1, Pallas kernels, body(): pl.pallas_call(functools.partial(layer_kernel, ring, snake), out_shape=ja...  43.3 us
    unnamed x1, local copies, waits for them, and re-layouts  1.57 us

profile of v7, /device:TPU:0, one launch (start us, length us, event | category | flops | bytes accessed | tf_op | source)
XLA Modules:
  0.0 44.9 jit_solution(13025128762940996102)
XLA Ops:
  0.0 43.3 %shard_map.100 = bf16[2,32,1024]{2,1,0:T(8,128)(2,1)} custom-call(bf16[2,32,1024]{2,1,0:T(8,128)(2,1)} %bitcast.8, bf16[2,32,256]{2,1,0:T(8,128)(2,1)} %bitcast.10, bf16[2,1536,256]{2,1,0:T(8,128)(2,1)} %bitcast.6, s32[4]{0:T(128)} %prefix_ref.1, s32[4]{0:T(128)} %valid_ref.1, bf16[2,32,1024]{2,1,0:T(8,128)(2,1)} %bitcast.9, f32[1,8192]{1,0:T(1,128)} %bitcast.11, ...), custom_call_target="tpu_custom_call" | custom-call | flops 5637144576 | bytes 44040192 | tf_op jit(solution)/shard_map/pallas_call | solution.py:573
  43.3 1.6 %copy.12 = bf16[1,2,32,1024]{3,2,1,0:T(8,128)(2,1)} copy(bf16[1,2,32,1024]{3,2,1,0:T(8,128)(2,1)} %bitcast.7) | data formatting | bytes 262144
